TPU v7x, 256 devices: a whole 4x4x8 slice. The times are simulated.
256 devices in a mesh: chan: 64 (over z_lo, x, y, core), space: 4 (over z_hi).
Axes of the slice: x: 4, y: 4, z: 8 (z_hi: 4, z_lo: 2; z = z_hi * 2 + z_lo), core: 2. Of those that a mesh axis runs over, the one named last changes fastest.
Arguments:
- volume: float32 [96, 128, 64, 128], P(None, 'chan', 'space'), may hold values from -6 to 6
- filters: float32 [27, 9216], replicated, may hold values from -0.125 to 0.125
- offsets: float32 [96], replicated, may hold values from -3 to 3
- upstream: float32 [96, 128, 64, 128], P(None, 'chan', 'space'), may hold values from -6 to 6
Outputs:
- response: float32 [96, 128, 64, 128], P(None, 'chan', 'space')
- volume_grad: float32 [96, 128, 64, 128], P(None, 'chan', 'space')
- filter_grad: float32 [27, 9216], replicated
- offset_grad: float32 [96], replicated
All inputs are finite; a program needn't handle non-finite values.
Results may differ from a plain program's by a relative error of at most 0.0085.
Values may be sent and summed in bfloat16 or wider, within the bound.
A program may use at most 128 MiB of HBM per device.

v0:
```python
import math

import jax
import jax.numpy as jnp
from jax import lax
from jax.sharding import PartitionSpec as P


def extended_2(cells, sides, width):
    for axis, dim in sides:
        count = lax.axis_size(axis)
        ends = count - 1
        head = lax.slice_in_dim(cells, 0, width, axis=dim)
        tail = lax.slice_in_dim(cells, cells.shape[dim] - width, cells.shape[dim], axis=dim)
        cells = jnp.concatenate(
            [
                lax.ppermute(tail, axis, [(i, (i + 1) % count) for i in range(ends)]),
                cells,
                lax.ppermute(head, axis, [((i + 1) % count, i) for i in range(ends)]),
            ],
            axis=dim,
        )
    return cells


def stacked(field):
    extent = field.shape[3]
    padded = jnp.pad(field, ((0, 0), (0, 0), (0, 0), (1, 1)))
    return jnp.concatenate(
        [padded[:, :, :, offset_z : offset_z + extent] for offset_z in range(3)], axis=0
    )


def correlate(shifted, blocks, first_len, second_len):
    summed = None
    for tap_first in range(3):
        for tap_second in range(3):
            window = shifted[
                :, tap_first : tap_first + first_len, tap_second : tap_second + second_len, :
            ]
            product_term = jnp.einsum(
                "ko,kxyz->oxyz",
                blocks[tap_first, tap_second],
                window,
                preferred_element_type=jnp.float32,
            )
            summed = product_term if summed is None else summed + product_term
    return summed


def on_device(volume, filters, offsets, upstream):
    channels = volume.shape[0]
    outputs_count = upstream.shape[0]
    first_len = volume.shape[1]
    second_len = volume.shape[2]
    kernel = filters.astype(jnp.bfloat16).reshape(3, 3, 3, channels, outputs_count)
    forward_blocks = kernel.reshape(3, 3, 3 * channels, outputs_count)
    reverse_blocks = jnp.transpose(kernel[::-1, ::-1, ::-1], (0, 1, 2, 4, 3)).reshape(
        3, 3, 3 * outputs_count, channels
    )
    rounded = volume.astype(jnp.bfloat16)
    cotangent = upstream.astype(jnp.bfloat16)
    bias_view = offsets[:, None, None, None]
    extended = extended_2(rounded, (("chan", 1), ("space", 2)), 1)
    shifted_in = stacked(extended)
    response = correlate(shifted_in, forward_blocks, first_len, second_len) + bias_view
    grad_ext = extended_2(cotangent, (("chan", 1), ("space", 2)), 1)
    volume_grad = correlate(stacked(grad_ext), reverse_blocks, first_len, second_len)
    weight_terms = []
    for tap_first in range(3):
        for tap_second in range(3):
            window = shifted_in[
                :, tap_first : tap_first + first_len, tap_second : tap_second + second_len, :
            ]
            weight_terms.append(
                jnp.einsum("kxyz,oxyz->ko", window, cotangent, preferred_element_type=jnp.float32)
            )
    weight_part = jnp.stack(weight_terms).reshape(27, channels * outputs_count)
    bias_part = jnp.sum(cotangent, axis=(1, 2, 3), dtype=jnp.float32)
    weight_sum, bias_sum = lax.psum((weight_part, bias_part), ("chan", "space"))
    cell_count = (
        first_len * lax.axis_size("chan") * second_len * lax.axis_size("space") * volume.shape[3]
    )
    factor = 1.0 / math.sqrt(cell_count)
    return (response, volume_grad, weight_sum * factor, bias_sum * factor)


def solution(mesh):
    placed = (P(None, "chan", "space", None), P(), P(), P(None, "chan", "space", None))
    return jax.shard_map(
        on_device,
        mesh=mesh,
        in_specs=placed,
        out_specs=(P(None, "chan", "space", None), P(None, "chan", "space", None), P(), P()),
        check_vma=False,
    )
```

profile of v0, /device:TPU:1, one launch (start us, length us, event | category | flops | bytes accessed | tf_op | source)
XLA Modules:
  0.0 452.2 jit_solution(7435219723326084311)
XLA Ops:
  7.2 2.5 convert_reduce_fusion
  9.8 0.9 fusion.57
  10.7 4.7 %collective-permute-start.4 = (bf16[96,1,16,128]{3,0,2,1:T(8,128)(2,1)}, bf16[96,1,16,128]{3,0,2,1:T(8,128)(2,1)S(1)}, u32[]{:S(2)}, u32[]{:S(2)}) collective-permute-start(bf16[96,1,16,128]{3,0,2,1:T(8,128)(2,1)} %get-tuple-element.26), channel_id=1, source_target_pairs={{0,4},{4,8},{8,12},{12,16},{16,20},{20,24},{24,28},{28,32},{32,36}... | collective-permute-start | bytes 1179656 | tf_op jit(solution)/shard_map/ppermute | solution.py:17
  15.4 1.9 collective-permute-start.5
  17.4 0.9 copy.106
  18.3 0.9 fusion.58
  19.2 3.6 collective-permute-start
  22.9 1.9 collective-permute-start.1
  24.9 1.5 reshape.18
  26.4 2.0 reverse_bitcast_fusion
  28.4 1.5 reshape_reshape.3
  29.9 2.2 copy.46
  32.0 84.1 %psum.15 = f32[96]{0:T(128)S(1)} all-reduce(f32[96]{0:T(128)S(1)} %get-tuple-element.16), channel_id=1, replica_groups=mesh['chan'=64,'space'=4] {'chan','space'}, use_global_device_ids=true, to_apply=%region_2.3 | all-reduce | flops 96 | bytes 768 | tf_op jit(solution)/shard_map/psum | solution.py:80
  116.6 0.8 pad_maximum_fusion.4
  117.4 1.9 collective-permute-start.6
  119.3 1.3 collective-permute-start.7
  120.7 4.9 %collective-permute-start.2 = (bf16[96,4,1,128]{3,0,2,1:T(8,128)(2,1)S(1)}, bf16[96,4,1,128]{3,0,2,1:T(8,128)(2,1)S(1)}, u32[]{:S(2)}, u32[]{:S(2)}) collective-permute-start(bf16[96,4,1,128]{3,0,2,1:T(8,128)(2,1)S(1)} %get-tuple-element.24), channel_id=1, source_target_pairs={{0,1},{1,2},{2,3},{4,5},{5,6},{6,7},{8,9},{9,10},{10,11},{12,13},{... | collective-permute-start | bytes 294920 | tf_op jit(solution)/shard_map/ppermute | solution.py:17
  125.6 1.5 collective-permute-start.3
  127.1 4.2 select_maximum_fusion
  131.3 0.9 fusion.55
  132.2 3.2 pad_maximum_fusion.1
  135.4 0.7 fusion.8
  141.0 3.3 select_maximum_fusion.4
  144.3 0.9 fusion.56
  145.2 5.9 %pad_maximum_fusion = bf16[288,4,18,128]{3,0,2,1:T(8,128)(2,1)S(1)} fusion(bf16[96,4,18,128]{3,0,2,1:T(8,128)(2,1)S(1)} %get-tuple-element.21, bf16[96,4,1,128]{3,0,2,1:T(8,128)(2,1)S(1)} %collective-permute-done.3, bf16[96,1,16,128]{3,0,2,1:T(8,128)(2,1)S(1)} %collective-permute-done.1, bf16[96,2,16,128]{3,0,2,1:T(8,128)(2,1)S(1)} %copy.106, ...), kind=kLoop, calls=%fused_computation.3 | loop fusion | flops 37158912 | bytes 10616832 | tf_op jit(solution)/shard_map/concatenate | solution.py:29
  151.2 1.9 fusion.50
  153.8 1.9 fusion.28
  155.6 1.9 fusion.30
  157.5 1.9 fusion.32
  159.4 1.9 fusion.34
  161.4 1.9 fusion.36
  163.2 1.8 fusion.38
  165.0 2.0 fusion.40
  167.0 1.2 add_bitcast_fusion.1
  168.2 2.1 copy.57
  170.3 1.4 fusion.49
  171.7 1.4 fusion.48
  173.2 1.4 fusion.47
  174.6 1.4 fusion.46
  176.0 1.4 fusion.45
  177.4 1.4 fusion.44
  178.9 1.4 fusion.43
  180.3 1.4 fusion.42
  181.7 3.2 reshape.20
  184.9 6.0 %add_bitcast_fusion = f32[96,2,16,128]{3,0,2,1:T(8,128)S(1)} fusion(f32[2,16,128,96]{2,3,1,0:T(8,128)S(1)} %fusion.26, f32[2,16,128,96]{2,3,1,0:T(8,128)} %fusion.28, f32[2,16,128,96]{2,3,1,0:T(8,128)} %fusion.30, f32[2,16,128,96]{2,3,1,0:T(8,128)} %fusion.32, f32[2,16,128,96]{2,3,1,0:T(8,128)} %fusion.34, f32[2,16,128,96]{2,3,1,0:T(8,128)} %fusion.36, ...), kind=kOutput, calls=%fused_computation.54 | convolution fusion | flops 230031360 | bytes 16589184 | tf_op jit(solution)/shard_map/ko,kxyz->oxyz/dot_general | solution.py:41
  191.0 2.1 copy.56
  193.0 250.0 %all-reduce.4.cloned.1.call-done = f32[27,9216]{1,0:T(8,128)} async-done(((f32[27,9216]{1,0:T(8,128)}), f32[27,9216]{1,0:T(8,128)}) %all-reduce.4.cloned.1.call-update) | async-done | bytes 995344 | tf_op jit(solution)/shard_map/psum | solution.py:80
  443.0 2.4 broadcast_multiply_fusion
  (33 shorter events, 6.3 us)
Async XLA Ops:
  7.2 435.9 %all-reduce.4.cloned.1.call-start = ((), (), s32[]{:S(2)}) async-start(), calls=%async_computation | async-start | bytes 2359296 | tf_op jit(solution)/shard_map/psum | solution.py:80
  7.2 10.2 %copy-start.3 = (f32[96,2,16,128]{3,2,1,0:T(8,128)S(1)}, f32[96,2,16,128]{3,2,1,0:T(8,128)}, u32[]{:S(2)}) copy-start(f32[96,2,16,128]{3,2,1,0:T(8,128)} %param.4) | copy-start | bytes 4718596
  10.7 14.1 %copy-start.4 = (f32[27,9216]{1,0:T(8,128)S(1)}, f32[27,9216]{1,0:T(8,128)}, u32[]{:S(2)}) copy-start(f32[27,9216]{1,0:T(8,128)} %param.5) | copy-start | bytes 2985988
  10.7 105.9 %collective-permute-start.4 = (bf16[96,1,16,128]{3,0,2,1:T(8,128)(2,1)}, bf16[96,1,16,128]{3,0,2,1:T(8,128)(2,1)S(1)}, u32[]{:S(2)}, u32[]{:S(2)}) collective-permute-start(bf16[96,1,16,128]{3,0,2,1:T(8,128)(2,1)} %get-tuple-element.26), channel_id=1, source_target_pairs={{0,4},{4,8},{8,12},{12,16},{16,20},{20,24},{24,28},{28,32},{32,36}... | collective-permute-start | bytes 1179656 | tf_op jit(solution)/shard_map/ppermute | solution.py:17
  15.4 101.2 %collective-permute-start.5 = (bf16[96,1,16,128]{3,0,2,1:T(8,128)(2,1)}, bf16[96,1,16,128]{3,0,2,1:T(8,128)(2,1)}, u32[]{:S(2)}, u32[]{:S(2)}) collective-permute-start(bf16[96,1,16,128]{3,0,2,1:T(8,128)(2,1)} %get-tuple-element.27), channel_id=1, source_target_pairs={{4,0},{8,4},{12,8},{16,12},{20,16},{24,20},{28,24},{32,28},{36,32}... | collective-permute-start | bytes 1179656 | tf_op jit(solution)/shard_map/ppermute | solution.py:19
  19.2 101.4 %collective-permute-start = (bf16[96,1,16,128]{3,0,2,1:T(8,128)(2,1)}, bf16[96,1,16,128]{3,0,2,1:T(8,128)(2,1)S(1)}, u32[]{:S(2)}, u32[]{:S(2)}) collective-permute-start(bf16[96,1,16,128]{3,0,2,1:T(8,128)(2,1)} %get-tuple-element.28), channel_id=1, source_target_pairs={{0,4},{4,8},{8,12},{12,16},{16,20},{20,24},{24,28},{28,32},{32,36}... | collective-permute-start | bytes 1179656 | tf_op jit(solution)/shard_map/ppermute | solution.py:17
  22.9 97.8 %collective-permute-start.1 = (bf16[96,1,16,128]{3,0,2,1:T(8,128)(2,1)}, bf16[96,1,16,128]{3,0,2,1:T(8,128)(2,1)S(1)}, u32[]{:S(2)}, u32[]{:S(2)}) collective-permute-start(bf16[96,1,16,128]{3,0,2,1:T(8,128)(2,1)} %get-tuple-element.29), channel_id=1, source_target_pairs={{4,0},{8,4},{12,8},{16,12},{20,16},{24,20},{28,24},{32,28},{36,32}... | collective-permute-start | bytes 1179656 | tf_op jit(solution)/shard_map/ppermute | solution.py:19
  117.4 9.7 %collective-permute-start.6 = (bf16[96,4,1,128]{3,0,2,1:T(8,128)(2,1)S(1)}, bf16[96,4,1,128]{3,0,2,1:T(8,128)(2,1)S(1)}, u32[]{:S(2)}, u32[]{:S(2)}) collective-permute-start(bf16[96,4,1,128]{3,0,2,1:T(8,128)(2,1)S(1)} %get-tuple-element.22), channel_id=1, source_target_pairs={{0,1},{1,2},{2,3},{4,5},{5,6},{6,7},{8,9},{9,10},{10,11},{12,13},{... | collective-permute-start | bytes 294920 | tf_op jit(solution)/shard_map/ppermute | solution.py:17
  119.3 7.8 %collective-permute-start.7 = (bf16[96,4,1,128]{3,0,2,1:T(8,128)(2,1)S(1)}, bf16[96,4,1,128]{3,0,2,1:T(8,128)(2,1)S(1)}, u32[]{:S(2)}, u32[]{:S(2)}) collective-permute-start(bf16[96,4,1,128]{3,0,2,1:T(8,128)(2,1)S(1)} %get-tuple-element.23), channel_id=1, source_target_pairs={{1,0},{2,1},{3,2},{5,4},{6,5},{7,6},{9,8},{10,9},{11,10},{13,12},{... | collective-permute-start | bytes 294920 | tf_op jit(solution)/shard_map/ppermute | solution.py:19
  120.7 20.3 %collective-permute-start.2 = (bf16[96,4,1,128]{3,0,2,1:T(8,128)(2,1)S(1)}, bf16[96,4,1,128]{3,0,2,1:T(8,128)(2,1)S(1)}, u32[]{:S(2)}, u32[]{:S(2)}) collective-permute-start(bf16[96,4,1,128]{3,0,2,1:T(8,128)(2,1)S(1)} %get-tuple-element.24), channel_id=1, source_target_pairs={{0,1},{1,2},{2,3},{4,5},{5,6},{6,7},{8,9},{9,10},{10,11},{12,13},{... | collective-permute-start | bytes 294920 | tf_op jit(solution)/shard_map/ppermute | solution.py:17
  125.6 15.4 %collective-permute-start.3 = (bf16[96,4,1,128]{3,0,2,1:T(8,128)(2,1)S(1)}, bf16[96,4,1,128]{3,0,2,1:T(8,128)(2,1)S(1)}, u32[]{:S(2)}, u32[]{:S(2)}) collective-permute-start(bf16[96,4,1,128]{3,0,2,1:T(8,128)(2,1)S(1)} %get-tuple-element.25), channel_id=1, source_target_pairs={{1,0},{2,1},{3,2},{5,4},{6,5},{7,6},{9,8},{10,9},{11,10},{13,12},{... | collective-permute-start | bytes 294920 | tf_op jit(solution)/shard_map/ppermute | solution.py:19
  132.2 3.2 copy-start.1
  151.1 29.2 %copy-start = (bf16[288,4,18,128]{3,0,2,1:T(8,128)(2,1)}, bf16[288,4,18,128]{3,0,2,1:T(8,128)(2,1)S(1)}, u32[]{:S(2)}) copy-start(bf16[288,4,18,128]{3,0,2,1:T(8,128)(2,1)S(1)} %pad_maximum_fusion) | copy-start | bytes 15925252
  151.2 1.9 copy-start.2
  181.7 3.2 copy-start.5
Sparse Core Ops, SparseCore 0:
  185.0 257.9 all-reduce.3
where the time goes:
time: 455 us; the launch traced here: 452 us
  waiting for transfers between devices  250 us (55%)
  blocking collectives  84.1 us (18%)
  matrix products  40.1 us (9%)
  other arithmetic  22.8 us (5%)
  starting transfers between devices  21.8 us (5%)
  local copies, waits for them, and re-layouts  19.1 us (4%)
  between operations  14.3 us (3%)
    psum x1, waiting for transfers between devices, on_device(): weight_sum, bias_sum = lax.psum((weight_part, bias_part), ('chan', 'space'))  250 us
    psum x1, blocking collectives, on_device(): weight_sum, bias_sum = lax.psum((weight_part, bias_part), ('chan', 'space'))  84.1 us
    dot_general x18, matrix products, correlate(): jnp.einsum('ko,kxyz->oxyz', blocks[tap_first, tap_second], window, prefer...  26.8 us
    ppermute x4, starting transfers between devices, extended_2(): lax.ppermute(tail, axis, [(i, (i + 1) % count) for i in range(ends)])  15.2 us
    dot_general x9, matrix products, on_device(): jnp.einsum('kxyz,oxyz->ko', window, cotangent, preferred_element_type=jnp...  13.3 us
  transfers between devices with their start and end apart: 9, of which 1 were waited for; matrix products, arithmetic and copies ran while one was open for 7% of the time, Pallas kernels for 0%

commit v1 on v0

v1 whole, which is shorter than its diff:
```python
import functools
import math

import jax
import jax.numpy as jnp
from jax import lax
from jax.experimental import pallas as pl
from jax.experimental.pallas import tpu as pltpu
from jax.sharding import PartitionSpec as P

MESH = pl.DeviceIdType.MESH
C = 96
NXL = 2
NYL = 16
NZ = 128
GX, GY, GZ = 4, 4, 8
ROWS = 2048
HALF = ROWS // 2
PIECE = HALF // (GX * GY)
PART = PIECE // GZ
SIDES = [(dc, ds) for dc in (-1, 0, 1) for ds in (-1, 0, 1) if (dc, ds) != (0, 0)]
XY = [(dx, dy) for dx in (2, 1, 3, 0) for dy in (2, 1, 3, 0) if (dx, dy) != (0, 0)]


def body(factor, vol_hbm, up_hbm, wf_ref, wr_ref, off_ref, resp_ref, vgrad_ref, grads_ref,
         vbuf, ubuf, xs, cs, x3, acc, crecv, p2, xyrecv, zs, zrecv, zag, gath,
         load_sem, hsend, hrecv, csend, crsem, xysend, xyrsem, zsend, zrsem, gzsend, gzrsem,
         gxsend, gxrsem, fsend, frsem):
    chan = lax.axis_index("chan")
    space = lax.axis_index("space")
    nchan = 2 * GX * GY * 2
    nspace = GZ // 2
    core = lax.rem(chan, 2)
    cy = lax.rem(chan // 2, GY)
    cx = lax.rem(chan // (2 * GY), GX)
    zl = chan // (2 * GY * GX)
    cz = space * 2 + zl
    idx = cx * GY + cy

    def device(z, x, y, k):
        return {"chan": ((lax.rem(z, 2) * GX + x) * GY + y) * 2 + k, "space": z // 2}

    sibling = device(cz, cx, cy, 1 - core)
    neighbours = [
        {"chan": lax.rem(chan + dc + nchan, nchan), "space": lax.rem(space + ds + nspace, nspace)}
        for dc, ds in SIDES
    ]
    xy_peers = [(lax.rem(cx + dx, GX), lax.rem(cy + dy, GY)) for dx, dy in XY]
    z_peers = [lax.rem(cz + dz, GZ) for dz in range(1, GZ)]

    barrier = pltpu.get_barrier_semaphore()
    everyone = neighbours + [sibling]
    everyone += [device(cz, x, y, core) for x, y in xy_peers]
    everyone += [device(z, cx, cy, core) for z in z_peers]
    load_up = pltpu.make_async_copy(up_hbm, ubuf, load_sem.at[0])
    load_up.start()
    load_vol = pltpu.make_async_copy(vol_hbm, vbuf, load_sem.at[1])
    load_vol.start()
    for one in everyone:
        pl.semaphore_signal(barrier, inc=1, device_id=one, device_id_type=MESH)

    lane = lax.broadcasted_iota(jnp.int32, (C, NZ), 1)
    first, last = lane == 0, lane == NZ - 1

    load_up.wait()

    @pl.loop(0, NXL * NYL)
    def _(n):
        v = ubuf[pl.ds(n, C, stride=NXL * NYL), :]
        cs[n // NYL + 1, lax.rem(n, NYL) + 1] = v.astype(jnp.bfloat16)

    pl.semaphore_wait(barrier, len(everyone))

    def halo(field, which):
        copies = []
        for n, (dc, ds) in enumerate(SIDES):
            def span(d, width, far):
                if d == 0:
                    return pl.ds(1, width)
                if far:
                    return pl.ds(0 if d > 0 else width + 1, 1)
                return pl.ds(width if d > 0 else 1, 1)
            copies.append(pltpu.make_async_remote_copy(
                src_ref=field.at[span(dc, NXL, False), span(ds, NYL, False)],
                dst_ref=field.at[span(dc, NXL, True), span(ds, NYL, True)],
                send_sem=hsend.at[which, n],
                recv_sem=hrecv.at[which, n],
                device_id=neighbours[n],
                device_id_type=MESH,
            ))
        return copies

    def trim(field):
        @pl.when(chan == 0)
        def _():
            field[0] = jnp.zeros_like(field[0])

        @pl.when(chan == nchan - 1)
        def _():
            field[NXL + 1] = jnp.zeros_like(field[NXL + 1])

        @pl.when(space == 0)
        def _():
            field[:, 0] = jnp.zeros_like(field[:, 0])

        @pl.when(space == nspace - 1)
        def _():
            field[:, NYL + 1] = jnp.zeros_like(field[:, NYL + 1])

    cs_halo = halo(cs, 0)
    for copy in cs_halo:
        copy.start()

    load_vol.wait()

    @pl.loop(0, NXL * NYL)
    def _(n):
        i, j = n // NYL, lax.rem(n, NYL)
        v = vbuf[pl.ds(n, C, stride=NXL * NYL), :]
        rounded = v.astype(jnp.bfloat16)
        xs[i + 1, j + 1] = rounded
        x3[i, j, pl.ds(C, C)] = rounded
        x3[i, j, pl.ds(0, C)] = jnp.where(first, 0.0, pltpu.roll(v, 1, axis=1)).astype(jnp.bfloat16)
        x3[i, j, pl.ds(2 * C, C)] = jnp.where(last, 0.0, pltpu.roll(v, NZ - 1, axis=1)).astype(jnp.bfloat16)
        x3[i, j, pl.ds(3 * C, 16)] = jnp.ones((16, NZ), jnp.bfloat16)

    for copy in cs_halo:
        copy.wait_recv()
    trim(cs)
    xs_halo = halo(xs, 1)
    for copy in xs_halo:
        copy.start()

    acc[...] = jnp.zeros_like(acc)

    def window(field, i, j):
        return jnp.concatenate(
            [field[pl.ds(i, 3), pl.ds(j + k, 3)].reshape(9 * C, NZ) for k in range(2)], axis=1
        )

    @pl.loop(0, NXL * NYL // 2)
    def _(n):
        i, j = n // (NYL // 2), lax.rem(n, NYL // 2) * 2
        left = jnp.concatenate([x3[i, j], x3[i, j + 1]], axis=1)
        terms = lax.dot_general(
            left, window(cs, i, j), (((1,), (1,)), ((), ())), preferred_element_type=jnp.float32
        )
        terms = jnp.concatenate([terms, jnp.zeros((3 * C + 16, 32), jnp.float32)], axis=1)
        for t in range(7):
            acc[pl.ds(t * 3 * C, 3 * C)] += terms[: 3 * C, t * 128 : (t + 1) * 128]
        acc[pl.ds(7 * 3 * C, 16)] += terms[3 * C :, 384:512]

    def convolve(out, field, weights, toward, bias):
        def step(n):
            i, j = n // (NYL // 2), lax.rem(n, NYL // 2) * 2
            y = jnp.dot(weights[...], window(field, i, j), preferred_element_type=jnp.float32)
            for k in range(2):
                low, mid, high = (y[r * C : (r + 1) * C, k * NZ : (k + 1) * NZ] for r in toward)
                total = mid + jnp.where(first, 0.0, pltpu.roll(low, 1, axis=1))
                total = total + jnp.where(last, 0.0, pltpu.roll(high, NZ - 1, axis=1))
                if bias is not None:
                    total = total + bias
                out[pl.ds(i * NYL + j + k, C, stride=NXL * NYL), :] = total
        return step

    square = lax.broadcasted_iota(jnp.int32, (C, C), 0) == lax.broadcasted_iota(jnp.int32, (C, C), 1)
    bias = jnp.sum(jnp.where(square, off_ref[...], 0.0), axis=1, keepdims=True)
    data_step = convolve(vgrad_ref, cs, wr_ref, (2, 1, 0), None)
    forward_step = convolve(resp_ref, xs, wf_ref, (0, 1, 2), bias)

    to_sibling = pltpu.make_async_remote_copy(
        src_ref=acc.at[pl.ds(pl.multiple_of((1 - core) * HALF, HALF), HALF)],
        dst_ref=crecv, send_sem=csend, recv_sem=crsem, device_id=sibling, device_id_type=MESH,
    )
    to_sibling.start()
    pl.loop(0, 6)(data_step)
    to_sibling.wait_recv()

    @pl.loop(0, GX * GY)
    def _(n):
        at = pl.multiple_of(core * HALF + n * PIECE, PIECE)
        total = acc[pl.ds(at, PIECE)] + crecv[pl.ds(pl.multiple_of(n * PIECE, PIECE), PIECE)]
        p2[n] = total.astype(jnp.bfloat16)

    mine = pl.multiple_of(core * HALF + idx * PIECE, PIECE)
    zs[...] = acc[pl.ds(mine, PIECE)] + crecv[pl.ds(pl.multiple_of(idx * PIECE, PIECE), PIECE)]

    xy_copies = []
    for n, (x, y) in enumerate(xy_peers):
        copy = pltpu.make_async_remote_copy(
            src_ref=p2.at[x * GY + y], dst_ref=xyrecv.at[n],
            send_sem=xysend.at[n], recv_sem=xyrsem.at[n],
            device_id=device(cz, x, y, core), device_id_type=MESH,
        )
        copy.start()
        xy_copies.append(copy)
    pl.loop(6, 16)(data_step)
    for n, copy in enumerate(xy_copies):
        copy.wait_recv()
    total = zs[...]
    for n in range(len(XY)):
        total = total + xyrecv[n].astype(jnp.float32)
    zs[...] = total

    z_copies = []
    for n, z in enumerate(z_peers):
        copy = pltpu.make_async_remote_copy(
            src_ref=zs.at[pl.ds(pl.multiple_of(z * PART, PART), PART)], dst_ref=zrecv.at[n],
            send_sem=zsend.at[n], recv_sem=zrsem.at[n],
            device_id=device(z, cx, cy, core), device_id_type=MESH,
        )
        copy.start()
        z_copies.append(copy)
    for copy in xs_halo:
        copy.wait_recv()
    trim(xs)
    pl.loop(0, 4)(forward_step)
    for copy in z_copies:
        copy.wait_recv()
    here = pl.ds(pl.multiple_of(cz * PART, PART), PART)
    total = zs[here]
    for n in range(len(z_peers)):
        total = total + zrecv[n]
    zag[here] = total * factor

    gz_copies = []
    for n, z in enumerate(z_peers):
        copy = pltpu.make_async_remote_copy(
            src_ref=zag.at[here], dst_ref=zag.at[here],
            send_sem=gzsend.at[n], recv_sem=gzrsem.at[n],
            device_id=device(z, cx, cy, core), device_id_type=MESH,
        )
        copy.start()
        gz_copies.append(copy)
    pl.loop(4, 8)(forward_step)
    for copy in gz_copies:
        copy.wait_recv()
    gath[core, idx] = zag[...].astype(jnp.bfloat16)

    gx_copies = []
    for n, (x, y) in enumerate(xy_peers):
        copy = pltpu.make_async_remote_copy(
            src_ref=gath.at[core, idx], dst_ref=gath.at[core, idx],
            send_sem=gxsend.at[n], recv_sem=gxrsem.at[n],
            device_id=device(cz, x, y, core), device_id_type=MESH,
        )
        copy.start()
        gx_copies.append(copy)

    def hand_on(n, source):
        return pltpu.make_async_remote_copy(
            src_ref=gath.at[core, source], dst_ref=gath.at[core, source],
            send_sem=fsend.at[n], recv_sem=frsem.at[n], device_id=sibling, device_id_type=MESH,
        )

    forwards = [hand_on(len(XY), idx)]
    forwards[0].start()
    pl.loop(8, 16)(forward_step)
    for n, (dx, dy) in enumerate(XY):
        gx_copies[n].wait_recv()
        source = lax.rem(cx - dx + GX, GX) * GY + lax.rem(cy - dy + GY, GY)
        forwards.append(hand_on(n, source))
        forwards[-1].start()
    for copy in forwards:
        copy.wait_recv()

    @pl.loop(0, GX * GY)
    def _(n):
        for k in range(2):
            grads_ref[pl.ds(pl.multiple_of(k * HALF + n * PIECE, PIECE), PIECE)] = gath[k, n].astype(jnp.float32)

    for copy in cs_halo + xs_halo + [to_sibling] + xy_copies + z_copies + gz_copies + gx_copies + forwards:
        copy.wait_send()


def on_device(volume, filters, offsets, upstream):
    cells = CELLS = volume.shape[1] * volume.shape[2] * volume.shape[3]
    cells = CELLS * lax.axis_size("chan") * lax.axis_size("space")
    factor = 1.0 / math.sqrt(cells)
    kernel = filters.astype(jnp.bfloat16).reshape(3, 3, 3, C, C)
    wf = jnp.transpose(kernel, (2, 4, 0, 1, 3)).reshape(3 * C, 9 * C)
    wr = jnp.transpose(kernel[::-1, ::-1], (2, 3, 0, 1, 4)).reshape(3 * C, 9 * C)
    flat = (C * NXL * NYL, NZ)
    f32, bf16 = jnp.float32, jnp.bfloat16
    vmem = pl.BlockSpec(memory_space=pltpu.VMEM)
    hbm = pl.BlockSpec(memory_space=pl.ANY)
    dma = pltpu.SemaphoreType.DMA
    resp, vgrad, grads = pl.pallas_call(
        functools.partial(body, factor),
        out_shape=[
            jax.ShapeDtypeStruct(flat, f32),
            jax.ShapeDtypeStruct(flat, f32),
            jax.ShapeDtypeStruct((ROWS, 128), f32),
        ],
        in_specs=[hbm, hbm, vmem, vmem, vmem],
        out_specs=[vmem, vmem, vmem],
        scratch_shapes=[
            pltpu.VMEM(flat, f32),
            pltpu.VMEM(flat, f32),
            pltpu.VMEM((NXL + 2, NYL + 2, C, NZ), bf16),
            pltpu.VMEM((NXL + 2, NYL + 2, C, NZ), bf16),
            pltpu.VMEM((NXL, NYL, 3 * C + 16, NZ), bf16),
            pltpu.VMEM((ROWS, 128), f32),
            pltpu.VMEM((HALF, 128), f32),
            pltpu.VMEM((GX * GY, PIECE, 128), bf16),
            pltpu.VMEM((GX * GY - 1, PIECE, 128), bf16),
            pltpu.VMEM((PIECE, 128), f32),
            pltpu.VMEM((GZ - 1, PART, 128), f32),
            pltpu.VMEM((PIECE, 128), f32),
            pltpu.VMEM((2, GX * GY, PIECE, 128), bf16),
            dma((2,)),
            dma((2, 8)),
            dma((2, 8)),
            dma,
            dma,
            dma((GX * GY - 1,)),
            dma((GX * GY - 1,)),
            dma((GZ - 1,)),
            dma((GZ - 1,)),
            dma((GZ - 1,)),
            dma((GZ - 1,)),
            dma((GX * GY - 1,)),
            dma((GX * GY - 1,)),
            dma((GX * GY,)),
            dma((GX * GY,)),
        ],
        compiler_params=pltpu.CompilerParams(
            collective_id=0, has_side_effects=True, vmem_limit_bytes=48 * 1024 * 1024
        ),
    )(volume.reshape(flat), upstream.reshape(flat), wf, wr, offsets.reshape(1, C))
    columns = jnp.concatenate([grads[t * 3 * C : (t + 1) * 3 * C] for t in range(7)], axis=1)[:, : 9 * C]
    taps = columns.reshape(3, C, 3, 3, C)[:, :, ::-1, ::-1]
    filter_grad = jnp.transpose(taps, (2, 3, 0, 1, 4)).reshape(27, C * C)
    offset_grad = grads[7 * 3 * C, :C]
    return (resp.reshape(volume.shape), vgrad.reshape(volume.shape), filter_grad, offset_grad)


def solution(mesh):
    placed = (P(None, "chan", "space", None), P(), P(), P(None, "chan", "space", None))
    return jax.shard_map(
        on_device,
        mesh=mesh,
        in_specs=placed,
        out_specs=(P(None, "chan", "space", None), P(None, "chan", "space", None), P(), P()),
        check_vma=False,
    )
```

time: 455 us -> 84.7 us (0.19)
  waiting for transfers between devices: 250 us -> 0 us
  blocking collectives: 84.1 us -> 0 us
  Pallas kernels: 0 us -> 57.9 us
  matrix products: 40.1 us -> 0 us
  starting transfers between devices: 21.8 us -> 0 us
  other arithmetic: 22.8 us -> 1.33 us
  between operations: 14.3 us -> 0.77 us
  local copies, waits for them, and re-layouts: 19.1 us -> 24.4 us
    psum x1 -> x0, waiting for transfers between devices: 250 us -> none  [on_device(): weight_sum, bias_sum = lax.psum((weight_part, bias_part), ('chan', 'space'))]
    psum x1 -> x0, blocking collectives: 84.1 us -> none  [on_device(): weight_sum, bias_sum = lax.psum((weight_part, bias_part), ('chan', 'space'))]
    pallas_call x0 -> x1, Pallas kernels: none -> 57.9 us  [on_device(): pl.pallas_call(functools.partial(body, factor), out_shape=[jax.ShapeDtype...]
    dot_general x27 -> x0, matrix products: 40.1 us -> none  [the longest x18 26.8 us: correlate(): jnp.einsum('ko,kxyz->oxyz', blocks[tap_first, tap_second], window, prefer...]
    ppermute x8 -> x0, starting transfers between devices: 21.8 us -> none  [the longest x4 15.2 us: extended_2(): lax.ppermute(tail, axis, [(i, (i + 1) % count) for i in range(ends)])]
    concatenate x4 -> x0, other arithmetic: 16.6 us -> none  [the longest x2 9.09 us: stacked(): jnp.concatenate([padded[:, :, :, offset_z:offset_z + extent] for offset_z...]
    rev x0 -> x2, local copies, waits for them, and re-layouts: none -> 10.7 us  [the longest x1 6.49 us: on_device(): taps = columns.reshape(3, C, 3, 3, C)[:, :, ::-1, ::-1]]
  transfers between devices with their start and end apart: 9 -> 0, of which waited for: 1 -> 0; matrix products, arithmetic and copies ran while one was open for 7% -> 0% of each run, Pallas kernels for 0% -> 0%
where the time goes in v1:
time: 84.7 us; the launch traced here: 84.4 us
  Pallas kernels  57.9 us (68%)
  local copies, waits for them, and re-layouts  24.4 us (29%)
  other arithmetic  1.33 us (2%)
    pallas_call x1, Pallas kernels, on_device(): pl.pallas_call(functools.partial(body, factor), out_shape=[jax.ShapeDtype...  57.9 us
    rev x1, local copies, waits for them, and re-layouts, on_device(): taps = columns.reshape(3, C, 3, 3, C)[:, :, ::-1, ::-1]  6.49 us
    rev x1, local copies, waits for them, and re-layouts, on_device(): kernel[::-1, ::-1]  4.18 us
    unnamed x14, local copies, waits for them, and re-layouts  3.51 us
    reshape x1, local copies, waits for them, and re-layouts, on_device(): filter_grad = jnp.transpose(taps, (2, 3, 0, 1, 4)).reshape(27, C * C)  3.28 us
    reshape x1, local copies, waits for them, and re-layouts, on_device(): taps = columns.reshape(3, C, 3, 3, C)[:, :, ::-1, ::-1]  2.17 us
    reshape x3, local copies, waits for them, and re-layouts, on_device(): kernel = filters.astype(jnp.bfloat16).reshape(3, 3, 3, C, C)  1.77 us

profile of v1, /device:TPU:1, one launch (start us, length us, event | category | flops | bytes accessed | tf_op | source)
XLA Modules:
  0.0 84.4 jit_solution(8215576125286840531)
XLA Ops:
  0.6 1.3 %convert_element_type.3 = bf16[27,9216]{1,0:T(8,128)(2,1)S(1)} convert(f32[27,9216]{1,0:T(8,128)} %param.5) | non-fusion elementwise | flops 248832 | bytes 1492992 | tf_op jit(solution)/shard_map/convert_element_type | solution.py:280
  2.0 0.7 reshape.40
  2.6 0.5 copy.14
  3.1 4.2 %rev.6 = bf16[3,3,3,96,96]{4,1,0,3,2:T(4,128)(2,1)S(1)} reverse(bf16[3,3,3,96,96]{4,1,0,3,2:T(4,128)(2,1)S(1)} %copy.14), dimensions={0,1} | reverse | bytes 995328 | tf_op jit(solution)/shard_map/rev | solution.py:282
  7.3 0.6 reshape.42.wr_ref
  7.9 0.0 copy-start.2
  7.9 0.7 copy.13
  8.6 0.6 reshape.41.wf_ref
  9.2 0.0 copy-done.2
  9.2 57.9 %shard_map.75 = (f32[3072,128]{1,0:T(8,128)S(1)}, f32[3072,128]{1,0:T(8,128)S(1)}, f32[2048,128]{1,0:T(8,128)S(1)}) custom-call(f32[3072,128]{1,0:T(8,128)} %bitcast.19, f32[3072,128]{1,0:T(8,128)} %bitcast.20, bf16[288,864]{1,0:T(8,128)(2,1)S(1)} %reshape.41.wf_ref, bf16[288,864]{1,0:T(8,128)(2,1)S(1)} %reshape.42.wr_ref, f32[1,96]{1,0:T(1,128)S(1)} %bitcast.15), custom_call_target="tpu_custom_call" | custom-call | tf_op jit(solution)/shard_map/pallas_call | solution.py:288
  67.1 0.0 copy-start
  67.1 1.1 %copy-done = f32[3072,128]{1,0:T(8,128)} copy-done((f32[3072,128]{1,0:T(8,128)}, f32[3072,128]{1,0:T(8,128)S(1)}, u32[]{:S(2)}) %copy-start) | copy-done | bytes 1572888
  68.3 0.5 slice_bitcast_fusion
  68.9 2.2 %reshape.46 = f32[3,96,3,3,96]{4,3,2,1,0:T(4,128)} reshape(f32[288,864]{1,0:T(8,128)S(1)} %bitcast.21) | data formatting | bytes 1990656 | tf_op jit(solution)/shard_map/reshape | solution.py:332
  71.1 6.5 %rev.7 = f32[3,96,3,3,96]{4,3,2,1,0:T(4,128)S(1)} reverse(f32[3,96,3,3,96]{4,3,2,1,0:T(4,128)} %reshape.46), dimensions={2,3} | reverse | bytes 1990656 | tf_op jit(solution)/shard_map/rev | solution.py:332
  77.6 1.2 %copy.15 = f32[3,3,3,96,96]{4,3,2,1,0:T(8,128)} copy(f32[3,3,3,96,96]{4,1,0,3,2:T(4,128)S(1)} %bitcast.16) | data formatting | bytes 1990656 | tf_op jit(solution)/shard_map/transpose | solution.py:333
  78.8 0.0 copy-start.1
  78.8 3.3 %reshape.47 = f32[27,9216]{1,0:T(8,128)} reshape(f32[3,3,3,96,96]{4,3,2,1,0:T(8,128)} %copy.15) | data formatting | bytes 1990656 | tf_op jit(solution)/shard_map/reshape | solution.py:333
  82.1 0.0 copy-done.1
  82.1 1.1 %copy.24 = f32[96,2,16,128]{3,2,1,0:T(8,128)} copy(f32[96,2,16,128]{3,2,1,0:T(8,128)S(1)} %bitcast.14) | data formatting | bytes 3145728
  83.3 1.1 %copy.25 = f32[96,2,16,128]{3,2,1,0:T(8,128)} copy(f32[96,2,16,128]{3,2,1,0:T(8,128)S(1)} %bitcast.13) | data formatting | bytes 3145728
  (7 shorter events, 0.1 us)
Async XLA Ops:
  7.9 1.3 %copy-start.2 = (f32[96]{0:T(128)S(1)}, f32[96]{0:T(128)}, u32[]{:S(2)}) copy-start(f32[96]{0:T(128)} %param.6) | copy-start | bytes 1156
  67.1 1.1 %copy-start = (f32[3072,128]{1,0:T(8,128)}, f32[3072,128]{1,0:T(8,128)S(1)}, u32[]{:S(2)}) copy-start(f32[3072,128]{1,0:T(8,128)S(1)} %get-tuple-element.7) | copy-start | bytes 4718596
  78.8 3.3 %copy-start.1 = (f32[3072,128]{1,0:T(8,128)S(1)}, f32[3072,128]{1,0:T(8,128)}, u32[]{:S(2)}) copy-start(f32[3072,128]{1,0:T(8,128)} %copy-done) | copy-start | bytes 4718596

commit v2 on v1

--- a/solution.py
+++ b/solution.py
@@ -22,8 +22,8 @@
 XY = [(dx, dy) for dx in (2, 1, 3, 0) for dy in (2, 1, 3, 0) if (dx, dy) != (0, 0)]
 
 
-def body(factor, vol_hbm, up_hbm, wf_ref, wr_ref, off_ref, resp_ref, vgrad_ref, grads_ref,
-         vbuf, ubuf, xs, cs, x3, acc, crecv, p2, xyrecv, zs, zrecv, zag, gath,
+def body(factor, vol_hbm, up_hbm, fbuf, off_ref, resp_ref, vgrad_ref, grads_ref,
+         vbuf, ubuf, fs, wf_ref, wr_ref, xs, cs, x3, acc, crecv, p2, xyrecv, zs, zrecv, zag, gath,
          load_sem, hsend, hrecv, csend, crsem, xysend, xyrsem, zsend, zrsem, gzsend, gzrsem,
          gxsend, gxrsem, fsend, frsem):
     chan = lax.axis_index("chan")
@@ -124,6 +124,18 @@
         x3[i, j, pl.ds(2 * C, C)] = jnp.where(last, 0.0, pltpu.roll(v, NZ - 1, axis=1)).astype(jnp.bfloat16)
         x3[i, j, pl.ds(3 * C, 16)] = jnp.ones((16, NZ), jnp.bfloat16)
 
+
+    @pl.loop(0, C // 4)
+    def _(n):
+        v = fbuf[:, pl.ds(pl.multiple_of(n * 4 * C, 128), 4 * C)]
+        for k in range(4):
+            fs[pl.ds(pl.multiple_of((n * 4 + k) * 32, 32), 27), :C] = v[:, k * C : (k + 1) * C]
+
+    for r in range(3):
+        taps = [fs[pl.ds(3 * n + r, C, stride=32), :][:, :C] for n in range(9)]
+        wr_ref[pl.ds(r * C, C), :] = jnp.concatenate(taps, axis=1).astype(jnp.bfloat16)
+        wf_ref[pl.ds(r * C, C), :] = jnp.concatenate([tap.T for tap in taps], axis=1).astype(jnp.bfloat16)
+
     for copy in cs_halo:
         copy.wait_recv()
     trim(cs)
@@ -133,9 +145,13 @@
 
     acc[...] = jnp.zeros_like(acc)
 
-    def window(field, i, j):
+    def window(field, i, j, order):
         return jnp.concatenate(
-            [field[pl.ds(i, 3), pl.ds(j + k, 3)].reshape(9 * C, NZ) for k in range(2)], axis=1
+            [
+                jnp.concatenate([field[i + p, j + k + q] for p in order for q in order], axis=0)
+                for k in range(2)
+            ],
+            axis=1,
         )
 
     @pl.loop(0, NXL * NYL // 2)
@@ -143,7 +159,7 @@
         i, j = n // (NYL // 2), lax.rem(n, NYL // 2) * 2
         left = jnp.concatenate([x3[i, j], x3[i, j + 1]], axis=1)
         terms = lax.dot_general(
-            left, window(cs, i, j), (((1,), (1,)), ((), ())), preferred_element_type=jnp.float32
+            left, window(cs, i, j, (2, 1, 0)), (((1,), (1,)), ((), ())), preferred_element_type=jnp.float32
         )
         terms = jnp.concatenate([terms, jnp.zeros((3 * C + 16, 32), jnp.float32)], axis=1)
         for t in range(7):
@@ -151,9 +167,11 @@
         acc[pl.ds(7 * 3 * C, 16)] += terms[3 * C :, 384:512]
 
     def convolve(out, field, weights, toward, bias):
+        order = toward
+
         def step(n):
             i, j = n // (NYL // 2), lax.rem(n, NYL // 2) * 2
-            y = jnp.dot(weights[...], window(field, i, j), preferred_element_type=jnp.float32)
+            y = jnp.dot(weights[...], window(field, i, j, order), preferred_element_type=jnp.float32)
             for k in range(2):
                 low, mid, high = (y[r * C : (r + 1) * C, k * NZ : (k + 1) * NZ] for r in toward)
                 total = mid + jnp.where(first, 0.0, pltpu.roll(low, 1, axis=1))
@@ -273,13 +291,37 @@
         copy.wait_send()
 
 
+def finish(resp_ref, vgrad_ref, grads_ref, resp_hbm, vgrad_hbm, filt_hbm, bias_ref, fs, fout, sem):
+    copies = [
+        pltpu.make_async_copy(resp_ref, resp_hbm, sem.at[0]),
+        pltpu.make_async_copy(vgrad_ref, vgrad_hbm, sem.at[1]),
+    ]
+    for copy in copies:
+        copy.start()
+    bias_ref[...] = grads_ref[pl.ds(7 * 3 * C, 1), :]
+    for r in range(3):
+        tiles = [grads_ref[pl.ds(t * 3 * C + r * C, C), :] for t in range(7)]
+        columns = jnp.concatenate(tiles, axis=1)
+        for n in range(9):
+            fs[pl.ds(3 * n + r, C, stride=32), :] = jnp.concatenate(
+                [columns[:, n * C : (n + 1) * C], jnp.zeros((C, 32), jnp.float32)], axis=1
+            )
+
+    @pl.loop(0, C // 4)
+    def _(n):
+        parts = [fs[pl.ds(pl.multiple_of((n * 4 + k) * 32, 32), 27), :][:, :C] for k in range(4)]
+        fout[:, pl.ds(pl.multiple_of(n * 4 * C, 128), 4 * C)] = jnp.concatenate(parts, axis=1)
+
+    last = pltpu.make_async_copy(fout, filt_hbm, sem.at[2])
+    last.start()
+    for copy in copies + [last]:
+        copy.wait()
+
+
 def on_device(volume, filters, offsets, upstream):
-    cells = CELLS = volume.shape[1] * volume.shape[2] * volume.shape[3]
-    cells = CELLS * lax.axis_size("chan") * lax.axis_size("space")
+    cells = volume.shape[1] * volume.shape[2] * volume.shape[3]
+    cells = cells * lax.axis_size("chan") * lax.axis_size("space")
     factor = 1.0 / math.sqrt(cells)
-    kernel = filters.astype(jnp.bfloat16).reshape(3, 3, 3, C, C)
-    wf = jnp.transpose(kernel, (2, 4, 0, 1, 3)).reshape(3 * C, 9 * C)
-    wr = jnp.transpose(kernel[::-1, ::-1], (2, 3, 0, 1, 4)).reshape(3 * C, 9 * C)
     flat = (C * NXL * NYL, NZ)
     f32, bf16 = jnp.float32, jnp.bfloat16
     vmem = pl.BlockSpec(memory_space=pltpu.VMEM)
@@ -292,11 +334,14 @@
             jax.ShapeDtypeStruct(flat, f32),
             jax.ShapeDtypeStruct((ROWS, 128), f32),
         ],
-        in_specs=[hbm, hbm, vmem, vmem, vmem],
+        in_specs=[hbm, hbm, vmem, vmem],
         out_specs=[vmem, vmem, vmem],
         scratch_shapes=[
             pltpu.VMEM(flat, f32),
             pltpu.VMEM(flat, f32),
+            pltpu.VMEM((C * 32, 128), f32),
+            pltpu.VMEM((3 * C, 9 * C), bf16),
+            pltpu.VMEM((3 * C, 9 * C), bf16),
             pltpu.VMEM((NXL + 2, NYL + 2, C, NZ), bf16),
             pltpu.VMEM((NXL + 2, NYL + 2, C, NZ), bf16),
             pltpu.VMEM((NXL, NYL, 3 * C + 16, NZ), bf16),
@@ -327,12 +372,21 @@
         compiler_params=pltpu.CompilerParams(
             collective_id=0, has_side_effects=True, vmem_limit_bytes=48 * 1024 * 1024
         ),
-    )(volume.reshape(flat), upstream.reshape(flat), wf, wr, offsets.reshape(1, C))
-    columns = jnp.concatenate([grads[t * 3 * C : (t + 1) * 3 * C] for t in range(7)], axis=1)[:, : 9 * C]
-    taps = columns.reshape(3, C, 3, 3, C)[:, :, ::-1, ::-1]
-    filter_grad = jnp.transpose(taps, (2, 3, 0, 1, 4)).reshape(27, C * C)
-    offset_grad = grads[7 * 3 * C, :C]
-    return (resp.reshape(volume.shape), vgrad.reshape(volume.shape), filter_grad, offset_grad)
+    )(volume.reshape(flat), upstream.reshape(flat), filters, offsets.reshape(1, C))
+    resp, vgrad, filter_grad, offset_grad = pl.pallas_call(
+        finish,
+        out_shape=[
+            jax.ShapeDtypeStruct(flat, f32),
+            jax.ShapeDtypeStruct(flat, f32),
+            jax.ShapeDtypeStruct((27, C * C), f32),
+            jax.ShapeDtypeStruct((1, 128), f32),
+        ],
+        in_specs=[vmem, vmem, vmem],
+        out_specs=[hbm, hbm, hbm, vmem],
+        scratch_shapes=[pltpu.VMEM((C * 32, 128), f32), pltpu.VMEM((27, C * C), f32), dma((3,))],
+        compiler_params=pltpu.CompilerParams(vmem_limit_bytes=16 * 1024 * 1024),
+    )(resp, vgrad, grads)
+    return (resp.reshape(volume.shape), vgrad.reshape(volume.shape), filter_grad, offset_grad[0, :C])
 
 
 def solution(mesh):

time: 84.7 us -> 62.8 us (0.74)
  local copies, waits for them, and re-layouts: 24.4 us -> 2.43 us
  Pallas kernels: 57.9 us -> 59.6 us
  other arithmetic: 1.33 us -> 0 us
    rev x2 -> x0, local copies, waits for them, and re-layouts: 10.7 us -> none  [the longest x1 6.49 us: on_device(): taps = columns.reshape(3, C, 3, 3, C)[:, :, ::-1, ::-1]]
    reshape x7 -> x0, local copies, waits for them, and re-layouts: 8.43 us -> none  [the longest x1 3.28 us: on_device(): filter_grad = jnp.transpose(taps, (2, 3, 0, 1, 4)).reshape(27, C * C)]
    pallas_call x0 -> x1, Pallas kernels: none -> 4.19 us  [on_device(): pl.pallas_call(finish, out_shape=[jax.ShapeDtypeStruct(flat, f32), jax.Sh...]
    pallas_call x1, Pallas kernels: 57.9 us -> 55.4 us  [on_device(): pl.pallas_call(functools.partial(body, factor), out_shape=[jax.ShapeDtype...]
    unnamed x14 -> x4, local copies, waits for them, and re-layouts: 3.51 us -> 1.92 us
    convert_element_type x1 -> x0, other arithmetic: 1.33 us -> none  [on_device(): kernel = filters.astype(jnp.bfloat16).reshape(3, 3, 3, C, C)]
    transpose x1 -> x0, local copies, waits for them, and re-layouts: 1.23 us -> none  [on_device(): filter_grad = jnp.transpose(taps, (2, 3, 0, 1, 4)).reshape(27, C * C)]
where the time goes in v2:
time: 62.8 us; the launch traced here: 62.7 us
  Pallas kernels  59.6 us (95%)
  local copies, waits for them, and re-layouts  2.43 us (4%)
  between operations  0.66 us (1%)
    pallas_call x1, Pallas kernels, on_device(): pl.pallas_call(functools.partial(body, factor), out_shape=[jax.ShapeDtype...  55.4 us
    pallas_call x1, Pallas kernels, on_device(): pl.pallas_call(finish, out_shape=[jax.ShapeDtypeStruct(flat, f32), jax.Sh...  4.19 us
    unnamed x4, local copies, waits for them, and re-layouts  1.92 us

profile of v2, /device:TPU:1, one launch (start us, length us, event | category | flops | bytes accessed | tf_op | source)
XLA Modules:
  0.0 62.7 jit_solution(18112508916170659338)
XLA Ops:
  0.6 0.0 copy-start
  0.6 1.3 %copy-done = f32[27,9216]{1,0:T(8,128)S(1)} copy-done((f32[27,9216]{1,0:T(8,128)S(1)}, f32[27,9216]{1,0:T(8,128)}, u32[]{:S(2)}) %copy-start) | copy-done | bytes 995352
  1.9 0.0 copy-start.1
  1.9 0.7 %copy-done.1 = f32[96]{0:T(128)S(1)} copy-done((f32[96]{0:T(128)S(1)}, f32[96]{0:T(128)}, u32[]{:S(2)}) %copy-start.1) | copy-done | bytes 408
  2.6 55.4 %shard_map.75 = (f32[3072,128]{1,0:T(8,128)S(1)}, f32[3072,128]{1,0:T(8,128)S(1)}, f32[2048,128]{1,0:T(8,128)S(1)}) custom-call(f32[3072,128]{1,0:T(8,128)} %bitcast.8, f32[3072,128]{1,0:T(8,128)} %bitcast.9, f32[27,9216]{1,0:T(8,128)S(1)} %copy-done, f32[1,96]{1,0:T(1,128)S(1)} %bitcast.7), custom_call_target="tpu_custom_call" | custom-call | tf_op jit(solution)/shard_map/pallas_call | solution.py:330
  58.0 4.2 %shard_map.76 = (f32[3072,128]{1,0:T(8,128)}, f32[3072,128]{1,0:T(8,128)}, f32[27,9216]{1,0:T(8,128)}, f32[1,128]{1,0:T(1,128)S(1)}) custom-call(f32[3072,128]{1,0:T(8,128)S(1)} %get-tuple-element.11.resp_ref, f32[3072,128]{1,0:T(8,128)S(1)} %get-tuple-element.12.vgrad_ref, f32[2048,128]{1,0:T(8,128)S(1)} %get-tuple-element.13.grads_ref), custom_call_target="tpu_custom_call" | custom-call | tf_op jit(solution)/shard_map/pallas_call | solution.py:376
  62.2 0.5 slice_bitcast_fusion
Async XLA Ops:
  0.6 1.3 %copy-start = (f32[27,9216]{1,0:T(8,128)S(1)}, f32[27,9216]{1,0:T(8,128)}, u32[]{:S(2)}) copy-start(f32[27,9216]{1,0:T(8,128)} %fbuf.1) | copy-start | bytes 2985988
  1.9 0.7 %copy-start.1 = (f32[96]{0:T(128)S(1)}, f32[96]{0:T(128)}, u32[]{:S(2)}) copy-start(f32[96]{0:T(128)} %param.6) | copy-start | bytes 1156

commit v3 on v0

v3 whole, which is shorter than its diff:
```python
import functools
import math

import jax
import jax.numpy as jnp
from jax import lax
from jax.experimental import pallas as pl
from jax.experimental.pallas import tpu as pltpu
from jax.sharding import PartitionSpec as P

MESH = pl.DeviceIdType.MESH
C = 96
NXL = 2
NYL = 16
NZ = 128
GX, GY, GZ = 4, 4, 8
TALL = 3 * C
ROWS = 2048
HALF = ROWS // 2
PIECE = HALF // (GX * GY)
BIAS = 7 * TALL
QS = (1, 0, 2)
HALVES = ((1, 9), (10, 7))
XY = [(dx, dy) for dx in (2, 1, 3, 0) for dy in (2, 1, 3, 0) if (dx, dy) != (0, 0)]
NT = (((1,), (1,)), ((), ()))


def body(factor, vol_hbm, up_hbm, filt_hbm, off_ref, resp0, resp1, vgrad0, vgrad1, gath,
         vbuf, ubuf, fbuf, fs, wf_ref, wr_ref, xs, cs, x3, acc, crecv, p2, xyrecv, own, zall,
         load_sem, hsend, hrecv, csend, crsem, xysend, xyrsem, zsend, zrsem,
         gxsend, gxrsem, fsend, frsem):
    f32, bf16 = jnp.float32, jnp.bfloat16
    chan = lax.axis_index("chan")
    space = lax.axis_index("space")
    nchan = 4 * GX * GY
    nspace = GZ // 2
    core = lax.rem(chan, 2)
    cy = lax.rem(chan // 2, GY)
    cx = lax.rem(chan // (2 * GY), GX)
    zl = chan // (2 * GY * GX)
    cz = space * 2 + zl
    idx = cx * GY + cy

    def device(z, x, y, k):
        return {"chan": ((lax.rem(z, 2) * GX + x) * GY + y) * 2 + k, "space": z // 2}

    def beside(dc, ds):
        return {"chan": lax.rem(chan + dc + nchan, nchan), "space": lax.rem(space + ds + nspace, nspace)}

    sibling = device(cz, cx, cy, 1 - core)
    xy_peers = [(lax.rem(cx + dx, GX), lax.rem(cy + dy, GY)) for dx, dy in XY]
    z_peers = [lax.rem(cz + dz, GZ) for dz in (4, 3, 5, 2, 6, 1, 7)]

    barrier = pltpu.get_barrier_semaphore()
    everyone = [beside(dc, ds) for dc in (-1, 1, 0) for ds in (-1, 1, 0) if (dc, ds) != (0, 0)]
    everyone += [sibling]
    everyone += [device(cz, x, y, core) for x, y in xy_peers]
    everyone += [device(z, cx, cy, core) for z in z_peers]
    load_up = pltpu.make_async_copy(up_hbm, ubuf, load_sem.at[0])
    load_up.start()
    for one in everyone:
        pl.semaphore_signal(barrier, inc=1, device_id=one, device_id_type=MESH)
    load_vol = pltpu.make_async_copy(vol_hbm, vbuf, load_sem.at[1])
    load_vol.start()
    load_filt = pltpu.make_async_copy(filt_hbm, fbuf, load_sem.at[2])
    load_filt.start()

    for field in (cs, xs):
        @pl.when(chan == 0)
        def _():
            field[0] = jnp.zeros((NYL + 2, C, NZ), bf16)

        @pl.when(chan == nchan - 1)
        def _():
            field[NXL + 1] = jnp.zeros((NYL + 2, C, NZ), bf16)

        @pl.when(space == 0)
        def _():
            for n in range(NXL + 2):
                field[n, 0] = jnp.zeros((C, NZ), bf16)

        @pl.when(space == nspace - 1)
        def _():
            for n in range(NXL + 2):
                field[n, NYL + 1] = jnp.zeros((C, NZ), bf16)

    lane = lax.broadcasted_iota(jnp.int32, (C, NZ), 1)
    first, last = lane == 0, lane == NZ - 1

    load_up.wait()

    @pl.loop(0, NXL * NYL, unroll=4)
    def _(n):
        v = ubuf[pl.ds(n, C, stride=NXL * NYL), :]
        cs[n // NYL + 1, lax.rem(n, NYL) + 1] = v.astype(bf16)

    pl.semaphore_wait(barrier, len(everyone))
    pending = []

    def inside(dc, ds):
        ok = None
        for d, at, count in ((dc, chan, nchan), (ds, space, nspace)):
            if d != 0:
                here = at < count - 1 if d > 0 else at > 0
                ok = here if ok is None else jnp.logical_and(ok, here)
        return ok

    class Halo:
        def __init__(self, field, which, n, dc, ds, row, count):
            plane_from, plane_to, planes = {-1: (1, NXL + 1, 1), 0: (1, 1, NXL), 1: (NXL, 0, 1)}[dc]
            row_from, row_to = {-1: (1, NYL + 1), 0: (row, row), 1: (NYL, 0)}[ds]
            self.copy = pltpu.make_async_remote_copy(
                src_ref=field.at[pl.ds(plane_from, planes), pl.ds(row_from, count)],
                dst_ref=field.at[pl.ds(plane_to, planes), pl.ds(row_to, count)],
                send_sem=hsend.at[which, n], recv_sem=hrecv.at[which, n],
                device_id=beside(dc, ds), device_id_type=MESH,
            )
            self.to, self.source = inside(dc, ds), inside(-dc, -ds)

        def start(self):
            pl.when(self.to)(self.copy.start)

        def wait_recv(self):
            pl.when(self.source)(self.copy.wait_recv)

        def wait_send(self):
            pl.when(self.to)(self.copy.wait_send)

    def halo(field, which):
        sides = [(dc, ds, 0, 1) for ds in (-1, 1) for dc in (0,)]
        sides += [(dc, ds, 0, 1) for dc in (-1, 1) for ds in (-1, 1)]
        sides += [(dc, 0, row, count) for row, count in HALVES for dc in (-1, 1)]
        return [Halo(field, which, n, *side) for n, side in enumerate(sides)]

    cs_halo = halo(cs, 0)
    for copy in cs_halo:
        copy.start()
    pending += cs_halo

    load_vol.wait()

    @pl.loop(0, NXL * NYL, unroll=4)
    def _(n):
        i, j = n // NYL, lax.rem(n, NYL)
        v = vbuf[pl.ds(n, C, stride=NXL * NYL), :]
        rounded = v.astype(bf16)
        xs[i + 1, j + 1] = rounded
        x3[i, j, pl.ds(C, C)] = rounded
        x3[i, j, pl.ds(0, C)] = jnp.where(first, 0.0, pltpu.roll(v, 1, axis=1)).astype(bf16)
        x3[i, j, pl.ds(2 * C, C)] = jnp.where(last, 0.0, pltpu.roll(v, NZ - 1, axis=1)).astype(bf16)
        x3[i, j, pl.ds(TALL, 16)] = jnp.ones((16, NZ), bf16)

    acc[pl.ds(6 * TALL, TALL)] = jnp.zeros((TALL, 128), f32)
    acc[pl.ds(BIAS, 32)] = jnp.zeros((32, 128), f32)
    step = NYL // 2

    def shifted(i, j):
        return jnp.concatenate([x3[i, j + k] for k in range(step)], axis=1)

    def terms(i, j, p, fresh):
        def rows(k):
            return jnp.concatenate([cs[i + 2 - p, j + k + 2 - q] for q in QS], axis=0)[:256]

        right = jnp.concatenate([rows(k) for k in range(step)], axis=1)
        v = lax.dot_general(shifted(i, j), right, NT, preferred_element_type=f32)
        for t in range(2):
            at = pl.ds((2 * p + t) * TALL, TALL)
            part = v[:TALL, t * 128 : (t + 1) * 128]
            acc[at] = part if fresh else acc[at] + part
        if p == 1:
            acc[pl.ds(BIAS, 16)] += v[TALL:, :128]

    def rest(i, j):
        def rows(k):
            return jnp.concatenate([cs[i + 2 - p, j + k + 2 - QS[2]][C - 32 :] for p in range(3)], axis=0)

        right = jnp.concatenate([rows(k) for k in range(step)], axis=1)
        v = lax.dot_general(shifted(i, j), right, NT, preferred_element_type=f32)
        acc[pl.ds(6 * TALL, TALL), : 3 * 32] += v[:TALL]

    rows_halo, corner_halo, plane_halo = cs_halo[:2], cs_halo[2:6], cs_halo[6:]
    for copy in rows_halo:
        copy.wait_recv()
    for j in (0, step):
        terms(0, j, 0, j == 0)
        terms(0, j, 1, j == 0)
        terms(1, j, 1, False)
        terms(1, j, 2, j == 0)

    load_filt.wait()

    for n in range(C // 4):
        v = fbuf[:, n * 4 * C : (n + 1) * 4 * C]
        for k in range(4):
            fs[pl.ds((n * 4 + k) * 32, 27), :C] = v[:, k * C : (k + 1) * C]
    for r in range(3):
        taps = [fs[pl.ds(3 * n + r, C, stride=32), :][:, :C] for n in range(9)]
        wr_ref[pl.ds(r * C, C), :] = jnp.concatenate(taps, axis=1).astype(bf16)
        wf_ref[pl.ds(r * C, C), :] = jnp.concatenate([tap.T for tap in taps], axis=1).astype(bf16)

    for copy in corner_halo + plane_halo[:2]:
        copy.wait_recv()
    xs_halo = halo(xs, 1)
    for part in range(2):
        if part == 1:
            for copy in plane_halo[2:]:
                copy.wait_recv()
            for copy in xs_halo:
                copy.start()
            pending += xs_halo
        j = part * step
        terms(0, j, 2, False)
        terms(1, j, 0, False)
        rest(0, j)
        rest(1, j)

    order = [x * GY + y for x, y in xy_peers] + [idx]
    core_copies = []
    for n, piece in enumerate(order):
        copy = pltpu.make_async_remote_copy(
            src_ref=acc.at[pl.ds(pl.multiple_of((1 - core) * HALF + piece * PIECE, PIECE), PIECE)],
            dst_ref=crecv.at[n], send_sem=csend.at[n], recv_sem=crsem.at[n],
            device_id=sibling, device_id_type=MESH,
        )
        copy.start()
        core_copies.append(copy)
    xy_copies = []
    for n, piece in enumerate(order):
        core_copies[n].wait_recv()
        total = acc[pl.ds(pl.multiple_of(core * HALF + piece * PIECE, PIECE), PIECE)] + crecv[n]
        if n == len(XY):
            own[...] = total
            break
        p2[n] = total.astype(bf16)
        x, y = xy_peers[n]
        copy = pltpu.make_async_remote_copy(
            src_ref=p2.at[n], dst_ref=xyrecv.at[n], send_sem=xysend.at[n], recv_sem=xyrsem.at[n],
            device_id=device(cz, x, y, core), device_id_type=MESH,
        )
        copy.start()
        xy_copies.append(copy)
    pending += core_copies + xy_copies

    def convolve(out, field, i, weights, order, bias):
        window = jnp.concatenate(
            [
                jnp.concatenate([field[i + p, k + q] for p in order for q in order], axis=0)
                for k in range(NYL)
            ],
            axis=1,
        )
        y = jnp.dot(weights[...], window, preferred_element_type=f32)
        for k in range(NYL):
            low, mid, high = (y[r * C : (r + 1) * C, k * NZ : (k + 1) * NZ] for r in order)
            total = mid + jnp.where(first, 0.0, pltpu.roll(low, 1, axis=1))
            total = total + jnp.where(last, 0.0, pltpu.roll(high, NZ - 1, axis=1))
            out[pl.ds(k, C, stride=NYL), :] = total if bias is None else total + bias

    convolve(vgrad0, cs, 0, wr_ref, (2, 1, 0), None)
    convolve(vgrad1, cs, 1, wr_ref, (2, 1, 0), None)

    for copy in xy_copies:
        copy.wait_recv()
    total = own[...]
    for n in range(len(XY)):
        total = total + xyrecv[n].astype(f32)

    zall[cz] = total.astype(bf16)
    z_copies = []
    for n, z in enumerate(z_peers):
        copy = pltpu.make_async_remote_copy(
            src_ref=zall.at[cz], dst_ref=zall.at[cz], send_sem=zsend.at[n], recv_sem=zrsem.at[n],
            device_id=device(z, cx, cy, core), device_id_type=MESH,
        )
        copy.start()
        z_copies.append(copy)
    pending += z_copies

    square = lax.broadcasted_iota(jnp.int32, (C, C), 0) == lax.broadcasted_iota(jnp.int32, (C, C), 1)
    bias = jnp.sum(jnp.where(square, off_ref[...], 0.0), axis=1, keepdims=True)
    for copy in xs_halo:
        copy.wait_recv()
    convolve(resp0, xs, 0, wf_ref, (0, 1, 2), bias)
    convolve(resp1, xs, 1, wf_ref, (0, 1, 2), bias)

    for copy in z_copies:
        copy.wait_recv()
    total = zall[0].astype(f32)
    for n in range(1, GZ):
        total = total + zall[n].astype(f32)
    gath[core, idx] = (total * factor).astype(bf16)

    def hand_on(n, source):
        return pltpu.make_async_remote_copy(
            src_ref=gath.at[core, source], dst_ref=gath.at[core, source],
            send_sem=fsend.at[n], recv_sem=frsem.at[n], device_id=sibling, device_id_type=MESH,
        )

    gx_copies = []
    for n, (x, y) in enumerate(xy_peers):
        copy = pltpu.make_async_remote_copy(
            src_ref=gath.at[core, idx], dst_ref=gath.at[core, idx],
            send_sem=gxsend.at[n], recv_sem=gxrsem.at[n],
            device_id=device(cz, x, y, core), device_id_type=MESH,
        )
        copy.start()
        gx_copies.append(copy)
    forwards = [hand_on(len(XY), idx)]
    forwards[0].start()
    for n, (dx, dy) in reversed(list(enumerate(XY))):
        gx_copies[n].wait_recv()
        source = lax.rem(cx - dx + GX, GX) * GY + lax.rem(cy - dy + GY, GY)
        forwards.append(hand_on(n, source))
        forwards[-1].start()
    for copy in forwards:
        copy.wait_recv()
    for copy in pending + gx_copies + forwards:
        copy.wait_send()


def finish(resp0, resp1, vgrad0, vgrad1, gath, resp_hbm, vgrad_hbm, filt_hbm, bias_ref, fs, fout, sem):
    copies = []
    for n, (source, out) in enumerate(
        ((resp0, resp_hbm), (resp1, resp_hbm), (vgrad0, vgrad_hbm), (vgrad1, vgrad_hbm))
    ):
        copies.append(pltpu.make_async_copy(source, out.at[:, n % 2], sem.at[n]))
        copies[-1].start()

    def rows(at):
        return gath[pl.ds(at, C), :].astype(jnp.float32)

    bias_ref[...] = gath[pl.ds(BIAS, 16), :].astype(jnp.float32)[:1, :C]
    for r in range(3):
        for p in range(3):
            columns = jnp.concatenate(
                [rows(t * TALL + r * C) for t in (2 * p, 2 * p + 1)]
                + [rows(6 * TALL + r * C)[:, 32 * p : 32 * (p + 1)]],
                axis=1,
            )
            for n, q in enumerate(QS):
                fs[pl.ds(9 * p + 3 * q + r, C, stride=32), :C] = columns[:, n * C : (n + 1) * C]
    for part in range(3):
        for n in range(part * 8, part * 8 + 8):
            parts = [fs[pl.ds((n * 4 + k) * 32, 27), :][:, :C] for k in range(4)]
            fout[:, n * 4 * C : (n + 1) * 4 * C] = jnp.concatenate(parts, axis=1)
        columns = pl.ds(part * 32 * C, 32 * C)
        copies.append(pltpu.make_async_copy(fout.at[:, columns], filt_hbm.at[:, columns], sem.at[4 + part]))
        copies[-1].start()
    for copy in copies:
        copy.wait()


def on_device(volume, filters, offsets, upstream):
    cells = volume.shape[1] * volume.shape[2] * volume.shape[3]
    cells = cells * lax.axis_size("chan") * lax.axis_size("space")
    factor = 1.0 / math.sqrt(cells)
    flat = (C * NXL * NYL, NZ)
    plane = (C * NYL, NZ)
    grid = (NXL + 2, NYL + 2, C, NZ)
    peers, along = GX * GY - 1, GZ - 1
    f32, bf16 = jnp.float32, jnp.bfloat16
    vmem = pl.BlockSpec(memory_space=pltpu.VMEM)
    hbm = pl.BlockSpec(memory_space=pl.ANY)
    dma = pltpu.SemaphoreType.DMA
    resp0, resp1, vgrad0, vgrad1, gath = pl.pallas_call(
        functools.partial(body, factor),
        out_shape=[jax.ShapeDtypeStruct(plane, f32)] * 4
        + [jax.ShapeDtypeStruct((2, GX * GY, PIECE, 128), bf16)],
        in_specs=[hbm, hbm, hbm, vmem],
        out_specs=[vmem] * 5,
        scratch_shapes=[
            pltpu.VMEM(flat, f32),
            pltpu.VMEM(flat, f32),
            pltpu.VMEM((27, C * C), f32),
            pltpu.VMEM((C * 32, 128), f32),
            pltpu.VMEM((TALL, 9 * C), bf16),
            pltpu.VMEM((TALL, 9 * C), bf16),
            pltpu.VMEM(grid, bf16),
            pltpu.VMEM(grid, bf16),
            pltpu.VMEM((NXL, NYL, TALL + 16, NZ), bf16),
            pltpu.VMEM((ROWS, 128), f32),
            pltpu.VMEM((peers + 1, PIECE, 128), f32),
            pltpu.VMEM((peers, PIECE, 128), bf16),
            pltpu.VMEM((peers, PIECE, 128), bf16),
            pltpu.VMEM((PIECE, 128), f32),
            pltpu.VMEM((GZ, PIECE, 128), bf16),
            dma((3,)),
            dma((2, 10)),
            dma((2, 10)),
            dma((peers + 1,)),
            dma((peers + 1,)),
            dma((peers,)),
            dma((peers,)),
            dma((along,)),
            dma((along,)),
            dma((peers,)),
            dma((peers,)),
            dma((peers + 1,)),
            dma((peers + 1,)),
        ],
        compiler_params=pltpu.CompilerParams(
            collective_id=0, has_side_effects=True, vmem_limit_bytes=50 * 1024 * 1024
        ),
    )(volume.reshape(flat), upstream.reshape(flat), filters, offsets.reshape(1, C))
    finished = pl.pallas_call(
        finish,
        out_shape=[
            jax.ShapeDtypeStruct((C, NXL, NYL, NZ), f32),
            jax.ShapeDtypeStruct((C, NXL, NYL, NZ), f32),
            jax.ShapeDtypeStruct((27, C * C), f32),
            jax.ShapeDtypeStruct((1, C), f32),
        ],
        in_specs=[vmem] * 5,
        out_specs=[hbm, hbm, hbm, vmem],
        scratch_shapes=[pltpu.VMEM((C * 32, 128), f32), pltpu.VMEM((27, C * C), f32), dma((7,))],
        compiler_params=pltpu.CompilerParams(vmem_limit_bytes=16 * 1024 * 1024),
    )(*(one.reshape(C, NYL, NZ) for one in (resp0, resp1, vgrad0, vgrad1)), gath.reshape(ROWS, 128))
    resp, vgrad, filter_grad, offset_grad = finished
    return (resp, vgrad, filter_grad, offset_grad.reshape(C))


def solution(mesh):
    placed = (P(None, "chan", "space", None), P(), P(), P(None, "chan", "space", None))
    return jax.shard_map(
        on_device,
        mesh=mesh,
        in_specs=placed,
        out_specs=(P(None, "chan", "space", None), P(None, "chan", "space", None), P(), P()),
        check_vma=False,
    )
```

time: 455 us -> 50.2 us (0.11)
  waiting for transfers between devices: 250 us -> 0 us
  blocking collectives: 84.1 us -> 0 us
  Pallas kernels: 0 us -> 48.9 us
  matrix products: 40.1 us -> 0 us
  other arithmetic: 22.8 us -> 0 us
  starting transfers between devices: 21.8 us -> 0 us
  local copies, waits for them, and re-layouts: 19.1 us -> 0.65 us
  between operations: 14.3 us -> 0.65 us
    psum x1 -> x0, waiting for transfers between devices: 250 us -> none  [on_device(): weight_sum, bias_sum = lax.psum((weight_part, bias_part), ('chan', 'space'))]
    psum x1 -> x0, blocking collectives: 84.1 us -> none  [on_device(): weight_sum, bias_sum = lax.psum((weight_part, bias_part), ('chan', 'space'))]
    pallas_call x0 -> x2, Pallas kernels: none -> 48.9 us  [the longest x1 45.3 us: on_device(): pl.pallas_call(functools.partial(body, factor), out_shape=[jax.ShapeDtype...]
    dot_general x27 -> x0, matrix products: 40.1 us -> none  [the longest x18 26.8 us: correlate(): jnp.einsum('ko,kxyz->oxyz', blocks[tap_first, tap_second], window, prefer...]
    ppermute x8 -> x0, starting transfers between devices: 21.8 us -> none  [the longest x4 15.2 us: extended_2(): lax.ppermute(tail, axis, [(i, (i + 1) % count) for i in range(ends)])]
    concatenate x4 -> x0, other arithmetic: 16.6 us -> none  [the longest x2 9.09 us: stacked(): jnp.concatenate([padded[:, :, :, offset_z:offset_z + extent] for offset_z...]
    reshape x2 -> x0, local copies, waits for them, and re-layouts: 4.68 us -> none  [the longest x1 3.18 us: on_device(): weight_part = jnp.stack(weight_terms).reshape(27, channels * outputs_count)]
  transfers between devices with their start and end apart: 9 -> 0, of which waited for: 1 -> 0; matrix products, arithmetic and copies ran while one was open for 7% -> 0% of each run, Pallas kernels for 0% -> 0%
where the time goes in v3:
time: 50.2 us
  Pallas kernels  48.9 us (97%)
  local copies, waits for them, and re-layouts  0.65 us (1%)
  between operations  0.65 us (1%)
    pallas_call x1, Pallas kernels, on_device(): pl.pallas_call(functools.partial(body, factor), out_shape=[jax.ShapeDtype...  45.3 us
    pallas_call x1, Pallas kernels, on_device(): pl.pallas_call(finish, out_shape=[jax.ShapeDtypeStruct((C, NXL, NYL, NZ),...  3.53 us

profile of v3, /device:TPU:1, one launch (start us, length us, event | category | flops | bytes accessed | tf_op | source)
XLA Modules:
  0.0 50.2 jit_solution(4671096854103905088)
XLA Ops:
  0.6 0.0 copy-start
  0.6 0.6 %copy-done = f32[96]{0:T(128)S(1)} copy-done((f32[96]{0:T(128)S(1)}, f32[96]{0:T(128)}, u32[]{:S(2)}) %copy-start) | copy-done | bytes 408
  1.3 45.3 %shard_map.75 = (f32[1536,128]{1,0:T(8,128)S(1)}, f32[1536,128]{1,0:T(8,128)S(1)}, f32[1536,128]{1,0:T(8,128)S(1)}, f32[1536,128]{1,0:T(8,128)S(1)}, bf16[2,16,64,128]{3,2,1,0:T(8,128)(2,1)S(1)}) custom-call(f32[3072,128]{1,0:T(8,128)} %bitcast.15, f32[3072,128]{1,0:T(8,128)} %bitcast.16, f32[27,9216]{1,0:T(8,128)} %filt_hbm.1, f32[1,96]{1,0:T(1,128)S(1)} %bitcast.14), custom_call_target="tpu_custom_call" | custom-call | tf_op jit(solution)/shard_map/pallas_call | solution.py:365
  46.6 3.5 %shard_map.76 = (f32[96,2,16,128]{3,2,1,0:T(8,128)}, f32[96,2,16,128]{3,2,1,0:T(8,128)}, f32[27,9216]{1,0:T(8,128)}, f32[1,96]{1,0:T(1,128)}) custom-call(f32[96,16,128]{2,1,0:T(8,128)S(1)} %bitcast.9, f32[96,16,128]{2,1,0:T(8,128)S(1)} %bitcast.10, f32[96,16,128]{2,1,0:T(8,128)S(1)} %bitcast.11, f32[96,16,128]{2,1,0:T(8,128)S(1)} %bitcast.12, ...), custom_call_target="tpu_custom_call" | custom-call | tf_op jit(solution)/shard_map/pallas_call | solution.py:405
Async XLA Ops:
  0.6 0.7 %copy-start = (f32[96]{0:T(128)S(1)}, f32[96]{0:T(128)}, u32[]{:S(2)}) copy-start(f32[96]{0:T(128)} %param.6) | copy-start | bytes 1156

commit v4 on v3

--- a/solution.py
+++ b/solution.py
@@ -19,13 +19,13 @@
 HALF = ROWS // 2
 PIECE = HALF // (GX * GY)
 BIAS = 7 * TALL
-QS = (1, 0, 2)
+TAPS = 40
 HALVES = ((1, 9), (10, 7))
 XY = [(dx, dy) for dx in (2, 1, 3, 0) for dy in (2, 1, 3, 0) if (dx, dy) != (0, 0)]
 NT = (((1,), (1,)), ((), ()))
 
 
-def body(factor, vol_hbm, up_hbm, filt_hbm, off_ref, resp0, resp1, vgrad0, vgrad1, gath,
+def body(factor, vol_hbm, up_hbm, filt_hbm, resp0, resp1, vgrad0, vgrad1, gath,
          vbuf, ubuf, fbuf, fs, wf_ref, wr_ref, xs, cs, x3, acc, crecv, p2, xyrecv, own, zall,
          load_sem, hsend, hrecv, csend, crsem, xysend, xyrsem, zsend, zrsem,
          gxsend, gxrsem, fsend, frsem):
@@ -65,25 +65,6 @@
     load_filt = pltpu.make_async_copy(filt_hbm, fbuf, load_sem.at[2])
     load_filt.start()
 
-    for field in (cs, xs):
-        @pl.when(chan == 0)
-        def _():
-            field[0] = jnp.zeros((NYL + 2, C, NZ), bf16)
-
-        @pl.when(chan == nchan - 1)
-        def _():
-            field[NXL + 1] = jnp.zeros((NYL + 2, C, NZ), bf16)
-
-        @pl.when(space == 0)
-        def _():
-            for n in range(NXL + 2):
-                field[n, 0] = jnp.zeros((C, NZ), bf16)
-
-        @pl.when(space == nspace - 1)
-        def _():
-            for n in range(NXL + 2):
-                field[n, NYL + 1] = jnp.zeros((C, NZ), bf16)
-
     lane = lax.broadcasted_iota(jnp.int32, (C, NZ), 1)
     first, last = lane == 0, lane == NZ - 1
 
@@ -127,7 +108,7 @@
             pl.when(self.to)(self.copy.wait_send)
 
     def halo(field, which):
-        sides = [(dc, ds, 0, 1) for ds in (-1, 1) for dc in (0,)]
+        sides = [(0, ds, 0, 1) for ds in (-1, 1)]
         sides += [(dc, ds, 0, 1) for dc in (-1, 1) for ds in (-1, 1)]
         sides += [(dc, 0, row, count) for row, count in HALVES for dc in (-1, 1)]
         return [Halo(field, which, n, *side) for n, side in enumerate(sides)]
@@ -136,6 +117,25 @@
     for copy in cs_halo:
         copy.start()
     pending += cs_halo
+
+    for field in (cs, xs):
+        @pl.when(chan == 0)
+        def _():
+            field[0] = jnp.zeros((NYL + 2, C, NZ), bf16)
+
+        @pl.when(chan == nchan - 1)
+        def _():
+            field[NXL + 1] = jnp.zeros((NYL + 2, C, NZ), bf16)
+
+        @pl.when(space == 0)
+        def _():
+            for n in range(NXL + 2):
+                field[n, 0] = jnp.zeros((C, NZ), bf16)
+
+        @pl.when(space == nspace - 1)
+        def _():
+            for n in range(NXL + 2):
+                field[n, NYL + 1] = jnp.zeros((C, NZ), bf16)
 
     load_vol.wait()
 
@@ -159,7 +159,8 @@
 
     def terms(i, j, p, fresh):
         def rows(k):
-            return jnp.concatenate([cs[i + 2 - p, j + k + 2 - q] for q in QS], axis=0)[:256]
+            low, mid, high = (cs[i + 2 - p, j + k + 2 - q] for q in range(3))
+            return jnp.concatenate([mid, high[:32], low, high[32:64]], axis=0)
 
         right = jnp.concatenate([rows(k) for k in range(step)], axis=1)
         v = lax.dot_general(shifted(i, j), right, NT, preferred_element_type=f32)
@@ -172,7 +173,7 @@
 
     def rest(i, j):
         def rows(k):
-            return jnp.concatenate([cs[i + 2 - p, j + k + 2 - QS[2]][C - 32 :] for p in range(3)], axis=0)
+            return jnp.concatenate([cs[i + 2 - p, j + k][C - 32 :] for p in range(3)], axis=0)
 
         right = jnp.concatenate([rows(k) for k in range(step)], axis=1)
         v = lax.dot_general(shifted(i, j), right, NT, preferred_element_type=f32)
@@ -205,9 +206,6 @@
         if part == 1:
             for copy in plane_halo[2:]:
                 copy.wait_recv()
-            for copy in xs_halo:
-                copy.start()
-            pending += xs_halo
         j = part * step
         terms(0, j, 2, False)
         terms(1, j, 0, False)
@@ -239,9 +237,11 @@
         )
         copy.start()
         xy_copies.append(copy)
-    pending += core_copies + xy_copies
-
-    def convolve(out, field, i, weights, order, bias):
+    pending += core_copies + xy_copies + xs_halo
+    for copy in xs_halo[:8]:
+        copy.start()
+
+    def convolve(out, field, i, weights, order):
         window = jnp.concatenate(
             [
                 jnp.concatenate([field[i + p, k + q] for p in order for q in order], axis=0)
@@ -254,10 +254,10 @@
             low, mid, high = (y[r * C : (r + 1) * C, k * NZ : (k + 1) * NZ] for r in order)
             total = mid + jnp.where(first, 0.0, pltpu.roll(low, 1, axis=1))
             total = total + jnp.where(last, 0.0, pltpu.roll(high, NZ - 1, axis=1))
-            out[pl.ds(k, C, stride=NYL), :] = total if bias is None else total + bias
-
-    convolve(vgrad0, cs, 0, wr_ref, (2, 1, 0), None)
-    convolve(vgrad1, cs, 1, wr_ref, (2, 1, 0), None)
+            out[pl.ds(k, C, stride=NYL), :] = total
+
+    convolve(vgrad0, cs, 0, wr_ref, (2, 1, 0))
+    convolve(vgrad1, cs, 1, wr_ref, (2, 1, 0))
 
     for copy in xy_copies:
         copy.wait_recv()
@@ -275,13 +275,8 @@
         copy.start()
         z_copies.append(copy)
     pending += z_copies
-
-    square = lax.broadcasted_iota(jnp.int32, (C, C), 0) == lax.broadcasted_iota(jnp.int32, (C, C), 1)
-    bias = jnp.sum(jnp.where(square, off_ref[...], 0.0), axis=1, keepdims=True)
-    for copy in xs_halo:
-        copy.wait_recv()
-    convolve(resp0, xs, 0, wf_ref, (0, 1, 2), bias)
-    convolve(resp1, xs, 1, wf_ref, (0, 1, 2), bias)
+    for copy in xs_halo[8:]:
+        copy.start()
 
     for copy in z_copies:
         copy.wait_recv()
@@ -307,6 +302,10 @@
         gx_copies.append(copy)
     forwards = [hand_on(len(XY), idx)]
     forwards[0].start()
+    for copy in xs_halo:
+        copy.wait_recv()
+    convolve(resp0, xs, 0, wf_ref, (0, 1, 2))
+    convolve(resp1, xs, 1, wf_ref, (0, 1, 2))
     for n, (dx, dy) in reversed(list(enumerate(XY))):
         gx_copies[n].wait_recv()
         source = lax.rem(cx - dx + GX, GX) * GY + lax.rem(cy - dy + GY, GY)
@@ -318,34 +317,41 @@
         copy.wait_send()
 
 
-def finish(resp0, resp1, vgrad0, vgrad1, gath, resp_hbm, vgrad_hbm, filt_hbm, bias_ref, fs, fout, sem):
+def finish(off_ref, resp0, resp1, vgrad0, vgrad1, gath, resp_hbm, vgrad_hbm, filt_hbm, bias_ref,
+           out0, out1, column, fs, fout, sem):
     copies = []
-    for n, (source, out) in enumerate(
-        ((resp0, resp_hbm), (resp1, resp_hbm), (vgrad0, vgrad_hbm), (vgrad1, vgrad_hbm))
-    ):
-        copies.append(pltpu.make_async_copy(source, out.at[:, n % 2], sem.at[n]))
+
+    def send(source, out):
+        copies.append(pltpu.make_async_copy(source, out, sem.at[len(copies)]))
         copies[-1].start()
+
+    send(vgrad0, vgrad_hbm.at[:, 0])
+    send(vgrad1, vgrad_hbm.at[:, 1])
+    square = lax.broadcasted_iota(jnp.int32, (C, C), 0) == lax.broadcasted_iota(jnp.int32, (C, C), 1)
+    offset = jnp.sum(jnp.where(square, off_ref[...], 0.0), axis=1, keepdims=True)
+    column[...] = jnp.broadcast_to(offset, (C, NZ))
+    for n, (source, out) in enumerate(((resp0, out0), (resp1, out1))):
+        for c in range(C):
+            out[c] = source[c] + column[pl.ds(c, 1), :]
+        send(out, resp_hbm.at[:, n])
 
     def rows(at):
         return gath[pl.ds(at, C), :].astype(jnp.float32)
 
     bias_ref[...] = gath[pl.ds(BIAS, 16), :].astype(jnp.float32)[:1, :C]
     for r in range(3):
+        last = rows(6 * TALL + r * C)
         for p in range(3):
-            columns = jnp.concatenate(
-                [rows(t * TALL + r * C) for t in (2 * p, 2 * p + 1)]
-                + [rows(6 * TALL + r * C)[:, 32 * p : 32 * (p + 1)]],
-                axis=1,
-            )
-            for n, q in enumerate(QS):
-                fs[pl.ds(9 * p + 3 * q + r, C, stride=32), :C] = columns[:, n * C : (n + 1) * C]
+            mid, low = rows(2 * p * TALL + r * C), rows((2 * p + 1) * TALL + r * C)
+            high = jnp.concatenate([mid[:, C:], low[:, C:], last[:, 32 * p : 32 * (p + 1)]], axis=1)
+            for q, part in enumerate((low[:, :C], mid[:, :C], high)):
+                fs[pl.ds(9 * p + 3 * q + r, C, stride=TAPS), :C] = part
     for part in range(3):
         for n in range(part * 8, part * 8 + 8):
-            parts = [fs[pl.ds((n * 4 + k) * 32, 27), :][:, :C] for k in range(4)]
+            parts = [fs[pl.ds((n * 4 + k) * TAPS, 27), :][:, :C] for k in range(4)]
             fout[:, n * 4 * C : (n + 1) * 4 * C] = jnp.concatenate(parts, axis=1)
         columns = pl.ds(part * 32 * C, 32 * C)
-        copies.append(pltpu.make_async_copy(fout.at[:, columns], filt_hbm.at[:, columns], sem.at[4 + part]))
-        copies[-1].start()
+        send(fout.at[:, columns], filt_hbm.at[:, columns])
     for copy in copies:
         copy.wait()
 
@@ -366,7 +372,7 @@
         functools.partial(body, factor),
         out_shape=[jax.ShapeDtypeStruct(plane, f32)] * 4
         + [jax.ShapeDtypeStruct((2, GX * GY, PIECE, 128), bf16)],
-        in_specs=[hbm, hbm, hbm, vmem],
+        in_specs=[hbm, hbm, hbm],
         out_specs=[vmem] * 5,
         scratch_shapes=[
             pltpu.VMEM(flat, f32),
@@ -401,7 +407,7 @@
         compiler_params=pltpu.CompilerParams(
             collective_id=0, has_side_effects=True, vmem_limit_bytes=50 * 1024 * 1024
         ),
-    )(volume.reshape(flat), upstream.reshape(flat), filters, offsets.reshape(1, C))
+    )(volume.reshape(flat), upstream.reshape(flat), filters)
     finished = pl.pallas_call(
         finish,
         out_shape=[
@@ -410,11 +416,18 @@
             jax.ShapeDtypeStruct((27, C * C), f32),
             jax.ShapeDtypeStruct((1, C), f32),
         ],
-        in_specs=[vmem] * 5,
+        in_specs=[vmem] * 6,
         out_specs=[hbm, hbm, hbm, vmem],
-        scratch_shapes=[pltpu.VMEM((C * 32, 128), f32), pltpu.VMEM((27, C * C), f32), dma((7,))],
+        scratch_shapes=[
+            pltpu.VMEM((C, NYL, NZ), f32),
+            pltpu.VMEM((C, NYL, NZ), f32),
+            pltpu.VMEM((C, NZ), f32),
+            pltpu.VMEM((C * TAPS, 128), f32),
+            pltpu.VMEM((27, C * C), f32),
+            dma((7,)),
+        ],
         compiler_params=pltpu.CompilerParams(vmem_limit_bytes=16 * 1024 * 1024),
-    )(*(one.reshape(C, NYL, NZ) for one in (resp0, resp1, vgrad0, vgrad1)), gath.reshape(ROWS, 128))
+    )(offsets.reshape(1, C), *(one.reshape(C, NYL, NZ) for one in (resp0, resp1, vgrad0, vgrad1)), gath.reshape(ROWS, 128))
     resp, vgrad, filter_grad, offset_grad = finished
     return (resp, vgrad, filter_grad, offset_grad.reshape(C))
 

time: 50.2 us -> 47.5 us (0.946)
  Pallas kernels: 48.9 us -> 46.7 us
  local copies, waits for them, and re-layouts: 0.65 us -> 0.01 us
    pallas_call x1, Pallas kernels: 45.3 us -> 43.9 us  [on_device(): pl.pallas_call(functools.partial(body, factor), out_shape=[jax.ShapeDtype...]
    pallas_call x1, Pallas kernels: 3.53 us -> 2.86 us  [on_device(): pl.pallas_call(finish, out_shape=[jax.ShapeDtypeStruct((C, NXL, NYL, NZ),...]
    unnamed x2, local copies, waits for them, and re-layouts: 0.65 us -> 0.01 us
where the time goes in v4:
time: 47.5 us; the launch traced here: 47.4 us
  Pallas kernels  46.7 us (98%)
  between operations  0.66 us (1%)
    pallas_call x1, Pallas kernels, on_device(): pl.pallas_call(functools.partial(body, factor), out_shape=[jax.ShapeDtype...  43.9 us
    pallas_call x1, Pallas kernels, on_device(): pl.pallas_call(finish, out_shape=[jax.ShapeDtypeStruct((C, NXL, NYL, NZ),...  2.86 us

profile of v4, /device:TPU:1, one launch (start us, length us, event | category | flops | bytes accessed | tf_op | source)
XLA Modules:
  0.0 47.4 jit_solution(12140025966919856137)
XLA Ops:
  0.6 0.0 copy-start
  0.6 43.9 %shard_map.75 = (f32[1536,128]{1,0:T(8,128)S(1)}, f32[1536,128]{1,0:T(8,128)S(1)}, f32[1536,128]{1,0:T(8,128)S(1)}, f32[1536,128]{1,0:T(8,128)S(1)}, bf16[2,16,64,128]{3,2,1,0:T(8,128)(2,1)S(1)}) custom-call(f32[3072,128]{1,0:T(8,128)} %bitcast.15, f32[3072,128]{1,0:T(8,128)} %bitcast.16, f32[27,9216]{1,0:T(8,128)} %filt_hbm.1), custom_call_target="tpu_custom_call" | custom-call | tf_op jit(solution)/shard_map/pallas_call | solution.py:371
  44.5 0.0 copy-done
  44.5 2.9 %shard_map.76 = (f32[96,2,16,128]{3,2,1,0:T(8,128)}, f32[96,2,16,128]{3,2,1,0:T(8,128)}, f32[27,9216]{1,0:T(8,128)}, f32[1,96]{1,0:T(1,128)}) custom-call(f32[1,96]{1,0:T(1,128)S(1)} %bitcast.14, f32[96,16,128]{2,1,0:T(8,128)S(1)} %bitcast.9, f32[96,16,128]{2,1,0:T(8,128)S(1)} %bitcast.10, f32[96,16,128]{2,1,0:T(8,128)S(1)} %bitcast.11, ...), custom_call_target="tpu_custom_call" | custom-call | tf_op jit(solution)/shard_map/pallas_call | solution.py:411
Async XLA Ops:
  0.6 43.9 %copy-start = (f32[96]{0:T(128)S(1)}, f32[96]{0:T(128)}, u32[]{:S(2)}) copy-start(f32[96]{0:T(128)} %param.6) | copy-start | bytes 1156

commit v5 on v4

--- a/solution.py
+++ b/solution.py
@@ -21,7 +21,8 @@
 BIAS = 7 * TALL
 TAPS = 40
 HALVES = ((1, 9), (10, 7))
-XY = [(dx, dy) for dx in (2, 1, 3, 0) for dy in (2, 1, 3, 0) if (dx, dy) != (0, 0)]
+FAR = (2, 1, 3, 0)
+XY = [(dx, dy) for dx in FAR for dy in FAR if (dx, dy) != (0, 0)]
 NT = (((1,), (1,)), ((), ()))
 
 
@@ -212,32 +213,36 @@
         rest(0, j)
         rest(1, j)
 
-    order = [x * GY + y for x, y in xy_peers] + [idx]
     core_copies = []
-    for n, piece in enumerate(order):
+    for n, dx in enumerate(FAR):
+        at = pl.multiple_of(lax.rem(cx + dx, GX) * GY * PIECE, GY * PIECE)
         copy = pltpu.make_async_remote_copy(
-            src_ref=acc.at[pl.ds(pl.multiple_of((1 - core) * HALF + piece * PIECE, PIECE), PIECE)],
+            src_ref=acc.at[pl.ds((1 - core) * HALF + at, GY * PIECE)],
             dst_ref=crecv.at[n], send_sem=csend.at[n], recv_sem=crsem.at[n],
             device_id=sibling, device_id_type=MESH,
         )
         copy.start()
         core_copies.append(copy)
     xy_copies = []
-    for n, piece in enumerate(order):
+    for n, dx in enumerate(FAR):
         core_copies[n].wait_recv()
-        total = acc[pl.ds(pl.multiple_of(core * HALF + piece * PIECE, PIECE), PIECE)] + crecv[n]
-        if n == len(XY):
-            own[...] = total
-            break
-        p2[n] = total.astype(bf16)
-        x, y = xy_peers[n]
-        copy = pltpu.make_async_remote_copy(
-            src_ref=p2.at[n], dst_ref=xyrecv.at[n], send_sem=xysend.at[n], recv_sem=xyrsem.at[n],
-            device_id=device(cz, x, y, core), device_id_type=MESH,
-        )
-        copy.start()
-        xy_copies.append(copy)
-    pending += core_copies + xy_copies + xs_halo
+        x = lax.rem(cx + dx, GX)
+        for dy in FAR:
+            y = lax.rem(cy + dy, GY)
+            at = pl.multiple_of(core * HALF + (x * GY + y) * PIECE, PIECE)
+            total = acc[pl.ds(at, PIECE)] + crecv[n, pl.ds(pl.multiple_of(y * PIECE, PIECE), PIECE)]
+            if (dx, dy) == (0, 0):
+                own[...] = total
+                continue
+            m = XY.index((dx, dy))
+            p2[m] = total.astype(bf16)
+            copy = pltpu.make_async_remote_copy(
+                src_ref=p2.at[m], dst_ref=xyrecv.at[m], send_sem=xysend.at[m], recv_sem=xyrsem.at[m],
+                device_id=device(cz, x, y, core), device_id_type=MESH,
+            )
+            copy.start()
+            xy_copies.append(copy)
+    pending += core_copies
     for copy in xs_halo[:8]:
         copy.start()
 
@@ -259,6 +264,8 @@
     convolve(vgrad0, cs, 0, wr_ref, (2, 1, 0))
     convolve(vgrad1, cs, 1, wr_ref, (2, 1, 0))
 
+    for copy in pending:
+        copy.wait_send()
     for copy in xy_copies:
         copy.wait_recv()
     total = own[...]
@@ -274,22 +281,17 @@
         )
         copy.start()
         z_copies.append(copy)
-    pending += z_copies
     for copy in xs_halo[8:]:
         copy.start()
 
+    for copy in xy_copies:
+        copy.wait_send()
     for copy in z_copies:
         copy.wait_recv()
     total = zall[0].astype(f32)
     for n in range(1, GZ):
         total = total + zall[n].astype(f32)
     gath[core, idx] = (total * factor).astype(bf16)
-
-    def hand_on(n, source):
-        return pltpu.make_async_remote_copy(
-            src_ref=gath.at[core, source], dst_ref=gath.at[core, source],
-            send_sem=fsend.at[n], recv_sem=frsem.at[n], device_id=sibling, device_id_type=MESH,
-        )
 
     gx_copies = []
     for n, (x, y) in enumerate(xy_peers):
@@ -300,20 +302,27 @@
         )
         copy.start()
         gx_copies.append(copy)
-    forwards = [hand_on(len(XY), idx)]
-    forwards[0].start()
+    for copy in z_copies + xs_halo:
+        copy.wait_send()
     for copy in xs_halo:
         copy.wait_recv()
     convolve(resp0, xs, 0, wf_ref, (0, 1, 2))
     convolve(resp1, xs, 1, wf_ref, (0, 1, 2))
-    for n, (dx, dy) in reversed(list(enumerate(XY))):
-        gx_copies[n].wait_recv()
-        source = lax.rem(cx - dx + GX, GX) * GY + lax.rem(cy - dy + GY, GY)
-        forwards.append(hand_on(n, source))
-        forwards[-1].start()
+    forwards = []
+    for dx in (0, 1, 3, 2):
+        for n in range(len(XY)):
+            if XY[n][0] == dx:
+                gx_copies[n].wait_recv()
+        source = pl.ds(lax.rem(cx - dx + GX, GX) * GY, GY)
+        copy = pltpu.make_async_remote_copy(
+            src_ref=gath.at[core, source], dst_ref=gath.at[core, source],
+            send_sem=fsend.at[dx], recv_sem=frsem.at[dx], device_id=sibling, device_id_type=MESH,
+        )
+        copy.start()
+        forwards.append(copy)
     for copy in forwards:
         copy.wait_recv()
-    for copy in pending + gx_copies + forwards:
+    for copy in gx_copies + forwards:
         copy.wait_send()
 
 
@@ -385,7 +394,7 @@
             pltpu.VMEM(grid, bf16),
             pltpu.VMEM((NXL, NYL, TALL + 16, NZ), bf16),
             pltpu.VMEM((ROWS, 128), f32),
-            pltpu.VMEM((peers + 1, PIECE, 128), f32),
+            pltpu.VMEM((GX, GY * PIECE, 128), f32),
             pltpu.VMEM((peers, PIECE, 128), bf16),
             pltpu.VMEM((peers, PIECE, 128), bf16),
             pltpu.VMEM((PIECE, 128), f32),
@@ -393,16 +402,16 @@
             dma((3,)),
             dma((2, 10)),
             dma((2, 10)),
-            dma((peers + 1,)),
-            dma((peers + 1,)),
+            dma((GX,)),
+            dma((GX,)),
             dma((peers,)),
             dma((peers,)),
             dma((along,)),
             dma((along,)),
             dma((peers,)),
             dma((peers,)),
-            dma((peers + 1,)),
-            dma((peers + 1,)),
+            dma((GX,)),
+            dma((GX,)),
         ],
         compiler_params=pltpu.CompilerParams(
             collective_id=0, has_side_effects=True, vmem_limit_bytes=50 * 1024 * 1024

time: 47.5 us -> 46.4 us (0.977)
  Pallas kernels: 46.7 us -> 45.7 us
    pallas_call x1, Pallas kernels: 43.9 us -> 42.8 us  [on_device(): pl.pallas_call(functools.partial(body, factor), out_shape=[jax.ShapeDtype...]
where the time goes in v5:
time: 46.4 us; the launch traced here: 46.3 us
  Pallas kernels  45.7 us (98%)
  between operations  0.66 us (1%)
    pallas_call x1, Pallas kernels, on_device(): pl.pallas_call(functools.partial(body, factor), out_shape=[jax.ShapeDtype...  42.8 us
    pallas_call x1, Pallas kernels, on_device(): pl.pallas_call(finish, out_shape=[jax.ShapeDtypeStruct((C, NXL, NYL, NZ),...  2.86 us

profile of v5, /device:TPU:1, one launch (start us, length us, event | category | flops | bytes accessed | tf_op | source)
XLA Modules:
  0.0 46.3 jit_solution(8277991311820326464)
XLA Ops:
  0.6 0.0 copy-start
  0.6 42.8 %shard_map.75 = (f32[1536,128]{1,0:T(8,128)S(1)}, f32[1536,128]{1,0:T(8,128)S(1)}, f32[1536,128]{1,0:T(8,128)S(1)}, f32[1536,128]{1,0:T(8,128)S(1)}, bf16[2,16,64,128]{3,2,1,0:T(8,128)(2,1)S(1)}) custom-call(f32[3072,128]{1,0:T(8,128)} %bitcast.15, f32[3072,128]{1,0:T(8,128)} %bitcast.16, f32[27,9216]{1,0:T(8,128)} %filt_hbm.1), custom_call_target="tpu_custom_call" | custom-call | tf_op jit(solution)/shard_map/pallas_call | solution.py:380
  43.4 0.0 copy-done
  43.5 2.9 %shard_map.76 = (f32[96,2,16,128]{3,2,1,0:T(8,128)}, f32[96,2,16,128]{3,2,1,0:T(8,128)}, f32[27,9216]{1,0:T(8,128)}, f32[1,96]{1,0:T(1,128)}) custom-call(f32[1,96]{1,0:T(1,128)S(1)} %bitcast.14, f32[96,16,128]{2,1,0:T(8,128)S(1)} %bitcast.9, f32[96,16,128]{2,1,0:T(8,128)S(1)} %bitcast.10, f32[96,16,128]{2,1,0:T(8,128)S(1)} %bitcast.11, ...), custom_call_target="tpu_custom_call" | custom-call | tf_op jit(solution)/shard_map/pallas_call | solution.py:420
Async XLA Ops:
  0.6 42.8 %copy-start = (f32[96]{0:T(128)S(1)}, f32[96]{0:T(128)}, u32[]{:S(2)}) copy-start(f32[96]{0:T(128)} %param.6) | copy-start | bytes 1156

commit v6 on v5

--- a/solution.py
+++ b/solution.py
@@ -246,20 +246,20 @@
     for copy in xs_halo[:8]:
         copy.start()
 
-    def convolve(out, field, i, weights, order):
+    def convolve(out, field, i, weights, order, start=0, count=NYL):
         window = jnp.concatenate(
             [
-                jnp.concatenate([field[i + p, k + q] for p in order for q in order], axis=0)
-                for k in range(NYL)
+                jnp.concatenate([field[i + p, start + k + q] for p in order for q in order], axis=0)
+                for k in range(count)
             ],
             axis=1,
         )
         y = jnp.dot(weights[...], window, preferred_element_type=f32)
-        for k in range(NYL):
+        for k in range(count):
             low, mid, high = (y[r * C : (r + 1) * C, k * NZ : (k + 1) * NZ] for r in order)
             total = mid + jnp.where(first, 0.0, pltpu.roll(low, 1, axis=1))
             total = total + jnp.where(last, 0.0, pltpu.roll(high, NZ - 1, axis=1))
-            out[pl.ds(k, C, stride=NYL), :] = total
+            out[pl.ds(start + k, C, stride=NYL), :] = total
 
     convolve(vgrad0, cs, 0, wr_ref, (2, 1, 0))
     convolve(vgrad1, cs, 1, wr_ref, (2, 1, 0))
@@ -284,8 +284,13 @@
     for copy in xs_halo[8:]:
         copy.start()
 
-    for copy in xy_copies:
+    for copy in xy_copies + xs_halo[:8]:
         copy.wait_send()
+    for copy in xs_halo[:8]:
+        copy.wait_recv()
+    half = NYL // 2
+    convolve(resp0, xs, 0, wf_ref, (0, 1, 2), 0, half)
+    convolve(resp1, xs, 1, wf_ref, (0, 1, 2), 0, half)
     for copy in z_copies:
         copy.wait_recv()
     total = zall[0].astype(f32)
@@ -302,12 +307,12 @@
         )
         copy.start()
         gx_copies.append(copy)
-    for copy in z_copies + xs_halo:
+    for copy in z_copies + xs_halo[8:]:
         copy.wait_send()
-    for copy in xs_halo:
-        copy.wait_recv()
-    convolve(resp0, xs, 0, wf_ref, (0, 1, 2))
-    convolve(resp1, xs, 1, wf_ref, (0, 1, 2))
+    for copy in xs_halo[8:]:
+        copy.wait_recv()
+    convolve(resp0, xs, 0, wf_ref, (0, 1, 2), half, half)
+    convolve(resp1, xs, 1, wf_ref, (0, 1, 2), half, half)
     forwards = []
     for dx in (0, 1, 3, 2):
         for n in range(len(XY)):

time: 46.4 us -> 46.4 us (level)
  no operation moved by 1% of the time
where the time goes in v6:
time: 46.4 us; the launch traced here: 46.3 us
  Pallas kernels  45.7 us (98%)
  between operations  0.66 us (1%)
    pallas_call x1, Pallas kernels, on_device(): pl.pallas_call(functools.partial(body, factor), out_shape=[jax.ShapeDtype...  42.8 us
    pallas_call x1, Pallas kernels, on_device(): pl.pallas_call(finish, out_shape=[jax.ShapeDtypeStruct((C, NXL, NYL, NZ),...  2.86 us

profile of v6, /device:TPU:1, one launch (start us, length us, event | category | flops | bytes accessed | tf_op | source)
XLA Modules:
  0.0 46.3 jit_solution(17104373363171026327)
XLA Ops:
  0.6 0.0 copy-start
  0.6 42.8 %shard_map.75 = (f32[1536,128]{1,0:T(8,128)S(1)}, f32[1536,128]{1,0:T(8,128)S(1)}, f32[1536,128]{1,0:T(8,128)S(1)}, f32[1536,128]{1,0:T(8,128)S(1)}, bf16[2,16,64,128]{3,2,1,0:T(8,128)(2,1)S(1)}) custom-call(f32[3072,128]{1,0:T(8,128)} %bitcast.15, f32[3072,128]{1,0:T(8,128)} %bitcast.16, f32[27,9216]{1,0:T(8,128)} %filt_hbm.1), custom_call_target="tpu_custom_call" | custom-call | tf_op jit(solution)/shard_map/pallas_call | solution.py:385
  43.4 0.0 copy-done
  43.5 2.9 %shard_map.76 = (f32[96,2,16,128]{3,2,1,0:T(8,128)}, f32[96,2,16,128]{3,2,1,0:T(8,128)}, f32[27,9216]{1,0:T(8,128)}, f32[1,96]{1,0:T(1,128)}) custom-call(f32[1,96]{1,0:T(1,128)S(1)} %bitcast.14, f32[96,16,128]{2,1,0:T(8,128)S(1)} %bitcast.9, f32[96,16,128]{2,1,0:T(8,128)S(1)} %bitcast.10, f32[96,16,128]{2,1,0:T(8,128)S(1)} %bitcast.11, ...), custom_call_target="tpu_custom_call" | custom-call | tf_op jit(solution)/shard_map/pallas_call | solution.py:425
Async XLA Ops:
  0.6 42.8 %copy-start = (f32[96]{0:T(128)S(1)}, f32[96]{0:T(128)}, u32[]{:S(2)}) copy-start(f32[96]{0:T(128)} %param.6) | copy-start | bytes 1156

commit v7 on v6

--- a/solution.py
+++ b/solution.py
@@ -27,7 +27,7 @@
 
 
 def body(factor, vol_hbm, up_hbm, filt_hbm, resp0, resp1, vgrad0, vgrad1, gath,
-         vbuf, ubuf, fbuf, fs, wf_ref, wr_ref, xs, cs, x3, acc, crecv, p2, xyrecv, own, zall,
+         vbuf, ubuf, fbuf, fs, wf_ref, wr_ref, xs, cs, x3, acc, give, crecv, p2, xyrecv, own, zall,
          load_sem, hsend, hrecv, csend, crsem, xysend, xyrsem, zsend, zrsem,
          gxsend, gxrsem, fsend, frsem):
     f32, bf16 = jnp.float32, jnp.bfloat16
@@ -54,9 +54,8 @@
 
     barrier = pltpu.get_barrier_semaphore()
     everyone = [beside(dc, ds) for dc in (-1, 1, 0) for ds in (-1, 1, 0) if (dc, ds) != (0, 0)]
-    everyone += [sibling]
     everyone += [device(cz, x, y, core) for x, y in xy_peers]
-    everyone += [device(z, cx, cy, core) for z in z_peers]
+    everyone += [device(z, cx, cy, core) for z in [lax.rem(cz + dz, GZ) for dz in (4, 3, 5, 1, 7)]]
     load_up = pltpu.make_async_copy(up_hbm, ubuf, load_sem.at[0])
     load_up.start()
     for one in everyone:
@@ -215,10 +214,10 @@
 
     core_copies = []
     for n, dx in enumerate(FAR):
-        at = pl.multiple_of(lax.rem(cx + dx, GX) * GY * PIECE, GY * PIECE)
+        at = pl.multiple_of((1 - core) * HALF + lax.rem(cx + dx, GX) * GY * PIECE, GY * PIECE)
+        give[n] = acc[pl.ds(at, GY * PIECE)].astype(bf16)
         copy = pltpu.make_async_remote_copy(
-            src_ref=acc.at[pl.ds((1 - core) * HALF + at, GY * PIECE)],
-            dst_ref=crecv.at[n], send_sem=csend.at[n], recv_sem=crsem.at[n],
+            src_ref=give.at[n], dst_ref=crecv.at[n], send_sem=csend.at[n], recv_sem=crsem.at[n],
             device_id=sibling, device_id_type=MESH,
         )
         copy.start()
@@ -230,7 +229,8 @@
         for dy in FAR:
             y = lax.rem(cy + dy, GY)
             at = pl.multiple_of(core * HALF + (x * GY + y) * PIECE, PIECE)
-            total = acc[pl.ds(at, PIECE)] + crecv[n, pl.ds(pl.multiple_of(y * PIECE, PIECE), PIECE)]
+            take = crecv[n, pl.ds(pl.multiple_of(y * PIECE, PIECE), PIECE)].astype(f32)
+            total = acc[pl.ds(at, PIECE)] + take
             if (dx, dy) == (0, 0):
                 own[...] = total
                 continue
@@ -399,7 +399,8 @@
             pltpu.VMEM(grid, bf16),
             pltpu.VMEM((NXL, NYL, TALL + 16, NZ), bf16),
             pltpu.VMEM((ROWS, 128), f32),
-            pltpu.VMEM((GX, GY * PIECE, 128), f32),
+            pltpu.VMEM((GX, GY * PIECE, 128), bf16),
+            pltpu.VMEM((GX, GY * PIECE, 128), bf16),
             pltpu.VMEM((peers, PIECE, 128), bf16),
             pltpu.VMEM((peers, PIECE, 128), bf16),
             pltpu.VMEM((PIECE, 128), f32),

time: 46.4 us -> 46.4 us (level)
  no operation moved by 1% of the time
where the time goes in v7:
time: 46.4 us; the launch traced here: 46.3 us
  Pallas kernels  45.6 us (98%)
  between operations  0.66 us (1%)
    pallas_call x1, Pallas kernels, on_device(): pl.pallas_call(functools.partial(body, factor), out_shape=[jax.ShapeDtype...  42.8 us
    pallas_call x1, Pallas kernels, on_device(): pl.pallas_call(finish, out_shape=[jax.ShapeDtypeStruct((C, NXL, NYL, NZ),...  2.86 us

profile of v7, /device:TPU:1, one launch (start us, length us, event | category | flops | bytes accessed | tf_op | source)
XLA Modules:
  0.0 46.3 jit_solution(1354024652177784652)
XLA Ops:
  0.6 0.0 copy-start
  0.6 42.8 %shard_map.75 = (f32[1536,128]{1,0:T(8,128)S(1)}, f32[1536,128]{1,0:T(8,128)S(1)}, f32[1536,128]{1,0:T(8,128)S(1)}, f32[1536,128]{1,0:T(8,128)S(1)}, bf16[2,16,64,128]{3,2,1,0:T(8,128)(2,1)S(1)}) custom-call(f32[3072,128]{1,0:T(8,128)} %bitcast.15, f32[3072,128]{1,0:T(8,128)} %bitcast.16, f32[27,9216]{1,0:T(8,128)} %filt_hbm.1), custom_call_target="tpu_custom_call" | custom-call | tf_op jit(solution)/shard_map/pallas_call | solution.py:385
  43.4 0.0 copy-done
  43.4 2.9 %shard_map.76 = (f32[96,2,16,128]{3,2,1,0:T(8,128)}, f32[96,2,16,128]{3,2,1,0:T(8,128)}, f32[27,9216]{1,0:T(8,128)}, f32[1,96]{1,0:T(1,128)}) custom-call(f32[1,96]{1,0:T(1,128)S(1)} %bitcast.14, f32[96,16,128]{2,1,0:T(8,128)S(1)} %bitcast.9, f32[96,16,128]{2,1,0:T(8,128)S(1)} %bitcast.10, f32[96,16,128]{2,1,0:T(8,128)S(1)} %bitcast.11, ...), custom_call_target="tpu_custom_call" | custom-call | tf_op jit(solution)/shard_map/pallas_call | solution.py:426
Async XLA Ops:
  0.6 42.8 %copy-start = (f32[96]{0:T(128)S(1)}, f32[96]{0:T(128)}, u32[]{:S(2)}) copy-start(f32[96]{0:T(128)} %param.6) | copy-start | bytes 1156
